TPU v7x, 32 devices: a whole 2x2x4 slice. The times are simulated.
32 devices in a mesh: dp: 4 (over z), tensor: 4 (over x, core), context: 2 (over y).
Axes of the slice: x: 2, y: 2, z: 4, core: 2. Of those that a mesh axis runs over, the one named last changes fastest.
Arguments:
- inputs: bfloat16 [4, 4096, 256], P('dp', 'tensor', 'context'), may hold values from -6 to 6
- out_grad: bfloat16 [4, 4096, 256], P('dp', 'tensor', 'context'), may hold values from -6 to 6
- filters: float32 [256, 256], P('tensor', 'context'), may hold values from -0.375 to 0.375
- skip: float32 [4096], P('tensor'), may hold values from 0.5 to 1.5
Outputs:
- grad_input: bfloat16 [4, 4096, 256], P('dp', 'tensor', 'context')
- grad_filter: float32 [256, 256], P('tensor', 'context')
All inputs are finite; a program needn't handle non-finite values.
Results may differ from a plain program's by a relative error of at most 0.0034.
Values may be sent and summed in bfloat16 or wider, within the bound.
No kernel may reach another device: no remote copies, remote signals or barrier semaphores. Data moves between devices by JAX's collectives and lax.ppermute only.
A program may use at most 64 MiB of HBM per device.

v0:
```python
import math

import jax
import jax.numpy as jnp
import numpy as np
from jax import lax
from jax.experimental import pallas as pl
from jax.experimental.pallas import tpu as pltpu
from jax.sharding import PartitionSpec as P

GROUP = 16


exact_mode = lax.Precision.HIGHEST


def block_tables(tok):
    step = np.arange(tok)
    angle = np.pi / tok * np.outer(step, step + 0.5)
    forward = np.concatenate([np.cos(angle), -np.sin(angle)], axis=1)
    inverse = np.concatenate([np.cos(angle).T, -np.sin(angle).T], axis=0) / tok
    pair = []
    for table, axis in ((forward, 0), (inverse, 1)):
        high = table.astype(jnp.bfloat16)
        low = (table - high.astype(np.float64)).astype(jnp.bfloat16)
        pair.append(jnp.asarray(np.concatenate([high, low], axis=axis)))
    return pair


def matmul(left, right):
    return jnp.dot(left, right, preferred_element_type=jnp.float32)


def split(value):
    high = value.astype(jnp.bfloat16)
    return high, (value - high.astype(jnp.float32)).astype(jnp.bfloat16)


def forward_exact(block, forward):
    return matmul(jnp.concatenate([block, block], axis=1), forward)


def forward_float(value, forward):
    high, low = split(value)
    return forward_exact(high, forward) + matmul(low, forward[: value.shape[1]])


def inverse_float(spec, inverse):
    tok = spec.shape[1] // 2
    high, low = split(spec)
    both = matmul(high, inverse)
    return both[:, :tok] + both[:, tok:] + matmul(low, inverse[:, :tok])


def conj_mul(left, right):
    tok = left.shape[1] // 2
    left_re, left_im = left[:, :tok], left[:, tok:]
    right_re, right_im = right[:, :tok], right[:, tok:]
    return (
        left_re * right_re + left_im * right_im,
        left_re * right_im - left_im * right_re,
    )


def group_sum(value):
    rows, width = value.shape
    return value.reshape(rows // GROUP, GROUP, width).sum(axis=1)


def group_spread(value):
    rows, width = value.shape
    return jnp.broadcast_to(value[:, None, :], (rows, GROUP, width)).reshape(rows * GROUP, width)


def sign_row(tok):
    lane = lax.broadcasted_iota(jnp.int32, (1, tok), 1)
    return (1 - 2 * (lane % 2)).astype(jnp.float32)


def local_lag_kernel(in_ref, grad_ref, forward_ref, inverse_ref, part_ref, lag_ref, taps_ref):
    first = lax.axis_index("context") == 0
    chans, tok = in_ref.shape
    rows = GROUP * 8
    forward = forward_ref[...]
    for start in range(0, chans, rows):
        span = pl.ds(start, rows)
        groups = pl.ds(start // GROUP, rows // GROUP)
        in_spec = forward_exact(in_ref[span, :], forward)
        grad_spec = forward_exact(grad_ref[span, :], forward)
        lag_re, lag_im = conj_mul(in_spec, grad_spec)
        lag_ref[groups, :tok] = group_sum(lag_re)
        lag_ref[groups, tok:] = group_sum(lag_im)
        part_ref[span, :] = jnp.where(first, in_spec, grad_spec)
    taps_ref[...] = inverse_float(lag_ref[...], inverse_ref[...])


def cross_lag_kernel(moved_ref, part_ref, lag_ref, taps_ref, forward_ref, inverse_ref, out_ref, sum_ref):
    first = lax.axis_index("context") == 0
    chans, tok = moved_ref.shape
    rows = GROUP * 8
    forward = forward_ref[...]
    for start in range(0, chans, rows):
        span = pl.ds(start, rows)
        groups = pl.ds(start // GROUP, rows // GROUP)
        spec = forward_exact(moved_ref[span, :], forward)
        re, im = conj_mul(part_ref[span, :], spec)
        sum_ref[groups, :tok] = group_sum(re)
        sum_ref[groups, tok:] = group_sum(im)
    sign = sign_row(tok)
    re, im = sum_ref[:, :tok], sum_ref[:, tok:]
    total = jnp.concatenate(
        [
            jnp.where(first, lag_ref[:, :tok] + sign * im, re),
            jnp.where(first, lag_ref[:, tok:] - sign * re, -im),
        ],
        axis=1,
    )
    taps = inverse_float(total, inverse_ref[...])
    out_ref[...] = taps + jnp.where(first, taps_ref[...], 0.0)


def local_corr_kernel(grad_ref, own_ref, other_ref, forward_ref, inverse_ref, corr_ref, turn_ref, base_ref):
    first = lax.axis_index("context") == 0
    chans, tok = grad_ref.shape
    rows = GROUP * 8
    forward = forward_ref[...]
    inverse = inverse_ref[...]
    base = forward_float(jnp.where(first, own_ref[...], other_ref[...]), forward)
    tail = forward_float(jnp.where(first, other_ref[...], own_ref[...]), forward)
    base_ref[...] = base
    sign = sign_row(tok)
    turn_ref[:, :tok] = jnp.where(first, tail[:, :tok] - sign * base[:, tok:], 0.0)
    turn_ref[:, tok:] = jnp.where(first, tail[:, tok:] + sign * base[:, :tok], 0.0)
    for start in range(0, chans, rows):
        span = pl.ds(start, rows)
        groups = pl.ds(start // GROUP, rows // GROUP)
        spec = forward_exact(grad_ref[span, :], forward)
        prod = conj_mul(group_spread(base_ref[groups, :]), spec)
        corr_ref[span, :] = inverse_float(jnp.concatenate(prod, axis=1), inverse)


def cross_corr_kernel(moved_ref, grad_ref, skip_ref, corr_ref, turn_ref, forward_ref, inverse_ref, out_ref):
    chans, tok = moved_ref.shape
    rows = GROUP * 8
    forward = forward_ref[...]
    inverse = inverse_ref[...]
    for start in range(0, chans, rows):
        span = pl.ds(start, rows)
        groups = pl.ds(start // GROUP, rows // GROUP)
        spec = forward_exact(moved_ref[span, :], forward)
        prod = conj_mul(group_spread(turn_ref[groups, :]), spec)
        corr = corr_ref[span, :] + inverse_float(jnp.concatenate(prod, axis=1), inverse)
        corr = corr.astype(jnp.bfloat16).astype(jnp.float32)
        gain = jnp.broadcast_to(skip_ref[start // rows, :][None, :], (tok, rows)).T
        out_ref[span, :] = (corr + gain * grad_ref[span, :].astype(jnp.float32)).astype(jnp.bfloat16)


VMEM_SPEC = pl.BlockSpec(memory_space=pltpu.VMEM)


def call(kernel, out_shape, scratch, cost, *operands):
    return pl.pallas_call(
        kernel,
        out_shape=out_shape,
        in_specs=[VMEM_SPEC] * len(operands),
        out_specs=jax.tree.map(lambda _: VMEM_SPEC, out_shape),
        scratch_shapes=scratch,
        cost_estimate=pl.CostEstimate(flops=cost, bytes_accessed=cost // 256, transcendentals=0),
        compiler_params=pltpu.CompilerParams(vmem_limit_bytes=24 * 1024 * 1024),
    )(*operands)


def in_vmem(value):
    return pltpu.with_memory_space_constraint(value, pltpu.VMEM)


def paired(inputs, out_grad, filters, skip):
    chans, tok = inputs.shape[1:]
    groups = filters.shape[0]
    sequences = lax.axis_size("dp")
    first = lax.axis_index("context") == 0
    swap = [(0, 1), (1, 0)]
    forward, inverse = block_tables(tok)
    own_in, own_grad = inputs[0], out_grad[0]
    skip_rows = skip.reshape(-1, GROUP * 8)
    cost = 4 * chans * tok * tok

    other_filters = lax.ppermute(filters, "context", swap)
    moved = lax.ppermute(jnp.where(first, own_in, own_grad), "context", swap)
    part, lag, taps = call(
        local_lag_kernel,
        (
            pltpu.VMEM((chans, 2 * tok), jnp.float32),
            pltpu.VMEM((groups, 2 * tok), jnp.float32),
            pltpu.VMEM((groups, tok), jnp.float32),
        ),
        [],
        8 * cost,
        own_in, own_grad, forward, inverse,
    )
    other_taps = lax.ppermute(taps, "context", swap)
    corr, turn = call(
        local_corr_kernel,
        (
            pltpu.VMEM((chans, tok), jnp.float32),
            pltpu.VMEM((groups, 2 * tok), jnp.float32),
        ),
        [pltpu.VMEM((groups, 2 * tok), jnp.float32)],
        8 * cost,
        own_grad, filters, other_filters, forward, inverse,
    )
    total = call(
        cross_lag_kernel,
        pltpu.VMEM((groups, tok), jnp.float32),
        [pltpu.VMEM((groups, 2 * tok), jnp.float32)],
        8 * cost,
        in_vmem(moved), part, lag, other_taps, forward, inverse,
    )
    grad_input = call(
        cross_corr_kernel,
        jax.ShapeDtypeStruct((chans, tok), jnp.bfloat16),
        [],
        8 * cost,
        in_vmem(moved), own_grad, skip_rows, corr, turn, forward, inverse,
    )
    step = 1
    while step < sequences:
        total = total + lax.ppermute(total, "dp", [(i, i ^ step) for i in range(sequences)])
        step *= 2
    norm_scale = 1.0 / math.sqrt(sequences * GROUP * 2 * tok)
    return (grad_input[None], total * norm_scale)


def dft_tables(size_one, size_two):
    padded_len = size_one * size_two
    range_one = jnp.arange(size_one, dtype=jnp.int32)
    range_two = jnp.arange(size_two, dtype=jnp.int32)
    angle_one = (range_one[:, None] * range_one[None, :] % size_one).astype(jnp.float32) * (
        -2.0 * math.pi / size_one
    )
    angle_two = (range_two[:, None] * range_two[None, :] % size_two).astype(jnp.float32) * (
        -2.0 * math.pi / size_two
    )
    angle_turn = (range_one[:, None] * range_two[None, :] % padded_len).astype(jnp.float32) * (
        -2.0 * math.pi / padded_len
    )
    return (
        jnp.cos(angle_one),
        jnp.sin(angle_one),
        jnp.cos(angle_two),
        jnp.sin(angle_two),
        jnp.cos(angle_turn),
        jnp.sin(angle_turn),
    )


def left_mul(matrix, operand):
    return jnp.einsum("kj,mjl->mkl", matrix, operand, precision=exact_mode)


def right_mul(operand, matrix):
    return jnp.einsum("mkj,jl->mkl", operand, matrix, precision=exact_mode)


def forward_real(signal, tables):
    one_re, one_im, two_re, two_im, turn_re, turn_im = tables
    half_rows = signal.shape[1]
    step_re = left_mul(one_re[:, :half_rows], signal)
    step_im = left_mul(one_im[:, :half_rows], signal)
    mid_re = step_re * turn_re - step_im * turn_im
    mid_im = step_re * turn_im + step_im * turn_re
    spec_re = right_mul(mid_re, two_re) - right_mul(mid_im, two_im)
    spec_im = right_mul(mid_re, two_im) + right_mul(mid_im, two_re)
    return (spec_re, spec_im)


def inverse_real(spec_re, spec_im, tables, half_rows):
    one_re, one_im, two_re, two_im, turn_re, turn_im = tables
    back_re = right_mul(spec_re, two_re) + right_mul(spec_im, two_im)
    back_im = right_mul(spec_im, two_re) - right_mul(spec_re, two_im)
    mid_re = back_re * turn_re + back_im * turn_im
    mid_im = back_im * turn_re - back_re * turn_im
    padded_len = one_re.shape[0] * two_re.shape[0]
    return (
        left_mul(one_re[:half_rows], mid_re) + left_mul(one_im[:half_rows], mid_im)
    ) / padded_len


def owner_groups(owners, own_ch, own_grp):
    starts = jnp.arange(owners, dtype=jnp.int32)[:, None] * own_ch // GROUP
    return starts + jnp.arange(own_grp, dtype=jnp.int32)[None, :]


def owned(inputs, out_grad, filters, skip):
    tok_dev = inputs.shape[2]
    ch_dev = inputs.shape[1]
    grp_dev = filters.shape[0]
    owners = lax.axis_size("context")
    seq_len = tok_dev * owners
    padded_len = 2 * seq_len
    own_ch = ch_dev // owners
    own_grp = max(1, own_ch // GROUP)
    per_group = own_ch // own_grp
    size_one = 1 << (padded_len.bit_length() - 1) // 2
    while padded_len % size_one != 0:
        size_one = size_one // 2
    size_two = padded_len // size_one
    half_rows = size_one // 2
    tables = dft_tables(size_one, size_two)
    moved_in, moved_grad = (
        lax.all_to_all(inputs, "context", split_axis=1, concat_axis=2, tiled=True),
        lax.all_to_all(out_grad, "context", split_axis=1, concat_axis=2, tiled=True),
    )
    slot_groups = owner_groups(owners, own_ch, own_grp)
    pick_rows = (
        slot_groups[:, :, None] == jnp.arange(grp_dev, dtype=jnp.int32)[None, None, :]
    ).astype(jnp.float32)
    outgoing = jnp.einsum("ojg,gt->ojt", pick_rows, filters, precision=exact_mode)
    own_filter = lax.all_to_all(
        outgoing, "context", split_axis=0, concat_axis=2, tiled=True
    ).reshape(own_grp, seq_len)
    sig_in = moved_in[0].astype(jnp.float32).reshape(own_ch, half_rows, size_two)
    sig_grad = moved_grad[0].astype(jnp.float32).reshape(own_ch, half_rows, size_two)
    in_re, in_im = forward_real(sig_in, tables)
    grad_re, grad_im = forward_real(sig_grad, tables)
    filt_re, filt_im = forward_real(own_filter.reshape(own_grp, half_rows, size_two), tables)
    grad_re4 = grad_re.reshape(own_grp, per_group, size_one, size_two)
    grad_im4 = grad_im.reshape(own_grp, per_group, size_one, size_two)
    filt_re4 = filt_re[:, None]
    filt_im4 = filt_im[:, None]
    prod_re = (filt_re4 * grad_re4 + filt_im4 * grad_im4).reshape(own_ch, size_one, size_two)
    prod_im = (filt_re4 * grad_im4 - filt_im4 * grad_re4).reshape(own_ch, size_one, size_two)
    correlated = (
        inverse_real(prod_re, prod_im, tables, half_rows)
        .reshape(1, own_ch, seq_len)
        .astype(jnp.bfloat16)
    )
    returned = lax.all_to_all(correlated, "context", split_axis=2, concat_axis=1, tiled=True)
    grad_input = (
        returned.astype(jnp.float32) + skip[None, :, None] * out_grad.astype(jnp.float32)
    ).astype(jnp.bfloat16)
    in_re4 = in_re.reshape(own_grp, per_group, size_one, size_two)
    in_im4 = in_im.reshape(own_grp, per_group, size_one, size_two)
    lag_re = (in_re4 * grad_re4 + in_im4 * grad_im4).sum(axis=1)
    lag_im = (in_re4 * grad_im4 - in_im4 * grad_re4).sum(axis=1)
    own_terms = inverse_real(lag_re, lag_im, tables, half_rows).reshape(own_grp, seq_len)
    pieces = lax.all_to_all(
        own_terms.reshape(own_grp, owners, tok_dev),
        "context",
        split_axis=1,
        concat_axis=0,
        tiled=True,
    )
    row_groups = owner_groups(owners, own_ch, own_grp).reshape(-1)
    pick_sum = (jnp.arange(grp_dev, dtype=jnp.int32)[:, None] == row_groups[None, :]).astype(
        jnp.float32
    )
    local_sum = jnp.dot(pick_sum, pieces.reshape(owners * own_grp, tok_dev), precision=exact_mode)
    summed = lax.psum(local_sum, "dp")
    norm_scale = 1.0 / math.sqrt(lax.axis_size("dp") * GROUP * seq_len)
    return (grad_input, summed * norm_scale)


def per_device(inputs, out_grad, filters, skip):
    sequences = lax.axis_size("dp")
    halves = lax.axis_size("context") == 2 and inputs.shape[0] == 1
    if halves and sequences & (sequences - 1) == 0 and inputs.shape[1] % (GROUP * 8) == 0:
        return paired(inputs, out_grad, filters, skip)
    return owned(inputs, out_grad, filters, skip)


def solution(mesh):
    in_specs = (
        P("dp", "tensor", "context"),
        P("dp", "tensor", "context"),
        P("tensor", "context"),
        P("tensor"),
    )
    out_specs = (P("dp", "tensor", "context"), P("tensor", "context"))
    return jax.shard_map(
        per_device, mesh=mesh, in_specs=in_specs, out_specs=out_specs, check_vma=False
    )
```

profile of v0, /device:TPU:0, one launch (start us, length us, event | category | flops | bytes accessed | tf_op | source)
XLA Modules:
  0.0 22.5 jit_solution(1655079682542607674)
XLA Ops:
  0.6 0.0 copy-start
  0.6 0.0 copy-start.1
  0.7 0.0 copy-start.4
  0.7 0.0 copy-start.5
  0.7 1.1 %broadcast_select_fusion = bf16[1024,128]{1,0:T(8,128)(2,1)S(1)} fusion(pred[]{:T(512)S(6)} %eq.3, bf16[1,1024,128]{2,1,0:T(8,128)(2,1)} %param.7, bf16[1,1024,128]{2,1,0:T(8,128)(2,1)} %param.6), kind=kLoop, calls=%fused_computation | loop fusion | flops 131072 | bytes 786433 | tf_op jit(solution)/shard_map/jit(_where)/select_n | solution.py:189
  1.8 3.0 %collective-permute-start = (bf16[1024,128]{1,0:T(8,128)(2,1)S(1)}, bf16[1024,128]{1,0:T(8,128)(2,1)S(1)}, u32[]{:S(2)}, u32[]{:S(2)}) collective-permute-start(bf16[1024,128]{1,0:T(8,128)(2,1)S(1)} %broadcast_select_fusion), channel_id=1, source_target_pairs={{0,1},{1,0},{2,3},{3,2},{4,5},{5,4},{6,7},{7,6},{8,9},{9,8},{10,11... | collective-permute-start | bytes 786440 | tf_op jit(solution)/shard_map/ppermute | solution.py:189
  4.8 0.0 copy-done
  4.8 0.0 copy-done.1
  4.8 0.0 copy-done.4
  4.8 0.0 copy-done.5
  4.9 0.0 copy-start.2
  4.9 0.6 %shard_map.79 = (f32[1024,256]{1,0:T(8,128)S(1)}, f32[64,256]{1,0:T(8,128)S(1)}, f32[64,128]{1,0:T(8,128)S(1)}) custom-call(bf16[1024,128]{1,0:T(8,128)(2,1)S(1)} %bitcast.6, bf16[1024,128]{1,0:T(8,128)(2,1)S(1)} %bitcast.7, bf16[256,256]{1,0:T(8,128)(2,1)S(1)} %copy-done.4, bf16[256,256]{1,0:T(8,128)(2,1)S(1)} %copy-done.5), custom_call_target="tpu_custom_call" | custom-call | flops 536870912 | bytes 2097152 | tf_op jit(solution)/shard_map/pallas_call | solution.py:162
  5.5 0.1 collective-permute-start.2
  5.5 0.1 copy-done.2
  5.6 1.9 %collective-permute-start.1 = (f32[64,128]{1,0:T(8,128)S(1)}, f32[64,128]{1,0:T(8,128)S(1)}, u32[]{:S(2)}, u32[]{:S(2)}) collective-permute-start(f32[64,128]{1,0:T(8,128)S(1)} %copy-done.2), channel_id=1, source_target_pairs={{0,1},{1,0},{2,3},{3,2},{4,5},{5,4},{6,7},{7,6},{8,9},{9,8},{10,11... | collective-permute-start | bytes 98312 | tf_op jit(solution)/shard_map/ppermute | solution.py:188
  7.5 4.7 %collective-permute-done.2.taps_ref = f32[64,128]{1,0:T(8,128)S(1)} collective-permute-done((f32[64,128]{1,0:T(8,128)S(1)}, f32[64,128]{1,0:T(8,128)S(1)}, u32[]{:S(2)}, u32[]{:S(2)}) %collective-permute-start.2) | collective-permute-done | bytes 32800 | tf_op jit(solution)/shard_map/ppermute | solution.py:201
  12.2 0.0 collective-permute-done.moved_ref
  12.2 0.5 %shard_map.80 = f32[64,128]{1,0:T(8,128)S(1)} custom-call(bf16[1024,128]{1,0:T(8,128)(2,1)S(1)} %collective-permute-done.moved_ref, f32[1024,256]{1,0:T(8,128)S(1)} %get-tuple-element.9.part_ref, f32[64,256]{1,0:T(8,128)S(1)} %get-tuple-element.10.lag_ref, f32[64,128]{1,0:T(8,128)S(1)} %collective-permute-done.2.taps_ref, bf16[256,256]{1,0:T(8,128)(2,1)S(1)} %copy-done.4, ...), custom_call_target="tpu_custom_call" | custom-call | flops 536870912 | bytes 2097152 | tf_op jit(solution)/shard_map/pallas_call | solution.py:162
  12.8 1.8 %collective-permute-start.3 = (f32[64,128]{1,0:T(8,128)S(1)}, f32[64,128]{1,0:T(8,128)S(1)}, u32[]{:S(2)}, u32[]{:S(2)}) collective-permute-start(f32[64,128]{1,0:T(8,128)S(1)} %shard_map.80), channel_id=1, source_target_pairs={{0,8},{8,0},{16,24},{24,16},{1,9},{9,1},{17,25},{25,17},{2,10},{10... | collective-permute-start | bytes 98312 | tf_op jit(solution)/shard_map/ppermute | solution.py:228
  14.6 0.0 collective-permute-done.1.other_ref
  14.6 1.6 %shard_map.77 = (f32[1024,128]{1,0:T(8,128)S(1)}, f32[64,256]{1,0:T(8,128)S(1)}) custom-call(bf16[1024,128]{1,0:T(8,128)(2,1)S(1)} %bitcast.8, f32[64,128]{1,0:T(8,128)S(1)} %copy-done.2, f32[64,128]{1,0:T(8,128)S(1)} %collective-permute-done.1.other_ref, bf16[256,256]{1,0:T(8,128)(2,1)S(1)} %copy-done.4, bf16[256,256]{1,0:T(8,128)(2,1)S(1)} %copy-done.5), custom_call_target="tpu_custom_call" | custom-call | flops 536870912 | bytes 2097152 | tf_op jit(solution)/shard_map/pallas_call | solution.py:162
  16.2 0.5 %collective-permute-done.3 = f32[64,128]{1,0:T(8,128)S(1)} collective-permute-done((f32[64,128]{1,0:T(8,128)S(1)}, f32[64,128]{1,0:T(8,128)S(1)}, u32[]{:S(2)}, u32[]{:S(2)}) %collective-permute-start.3) | collective-permute-done | bytes 32800 | tf_op jit(solution)/shard_map/ppermute | solution.py:228
  16.7 0.0 copy-start.3
  16.7 2.9 %collective-permute-start.4 = (f32[64,128]{1,0:T(8,128)S(1)}, f32[64,128]{1,0:T(8,128)S(1)}, u32[]{:S(2)}, u32[]{:S(2)}) collective-permute-start(f32[64,128]{1,0:T(8,128)S(1)} %add.6), channel_id=1, source_target_pairs={{0,16},{8,24},{16,0},{24,8},{1,17},{9,25},{17,1},{25,9},{2,18},{10... | collective-permute-start | bytes 98312 | tf_op jit(solution)/shard_map/ppermute | solution.py:228
  19.6 0.0 copy-done.3
  19.6 2.2 %shard_map.78 = bf16[1024,128]{1,0:T(8,128)(2,1)} custom-call(bf16[1024,128]{1,0:T(8,128)(2,1)S(1)} %collective-permute-done.moved_ref, bf16[1024,128]{1,0:T(8,128)(2,1)S(1)} %bitcast.9, f32[8,128]{1,0:T(8,128)S(1)} %bitcast.10, f32[1024,128]{1,0:T(8,128)S(1)} %get-tuple-element.7.corr_ref, f32[64,256]{1,0:T(8,128)S(1)} %get-tuple-element.8.turn_ref, ...), custom_call_target="tpu_custom_call" | custom-call | flops 536870912 | bytes 2097152 | tf_op jit(solution)/shard_map/pallas_call | solution.py:162
  21.8 0.0 collective-permute-done.4
  21.8 0.6 %add_multiply_fusion = f32[64,128]{1,0:T(8,128)} fusion(f32[64,128]{1,0:T(8,128)S(1)} %add.6, f32[64,128]{1,0:T(8,128)S(1)} %collective-permute-done.4), kind=kLoop, calls=%fused_computation.1 | loop fusion | flops 16384 | bytes 98304 | tf_op jit(solution)/shard_map/mul | solution.py:231
  (1 shorter events, 0.0 us)
Async XLA Ops:
  0.6 4.2 %copy-start = (bf16[1,1024,128]{2,1,0:T(8,128)(2,1)S(1)}, bf16[1,1024,128]{2,1,0:T(8,128)(2,1)}, u32[]{:S(2)}) copy-start(bf16[1,1024,128]{2,1,0:T(8,128)(2,1)} %param.6) | copy-start | bytes 786436
  0.6 4.2 %copy-start.1 = (bf16[1,1024,128]{2,1,0:T(8,128)(2,1)S(1)}, bf16[1,1024,128]{2,1,0:T(8,128)(2,1)}, u32[]{:S(2)}) copy-start(bf16[1,1024,128]{2,1,0:T(8,128)(2,1)} %param.7) | copy-start | bytes 786436
  0.7 4.2 %copy-start.4 = (bf16[256,256]{1,0:T(8,128)(2,1)S(1)}, bf16[256,256]{1,0:T(8,128)(2,1)}, u32[]{:S(2)}) copy-start(bf16[256,256]{1,0:T(8,128)(2,1)} %constant.12.clone.forward_ref) | copy-start | bytes 393220
  0.7 4.2 %copy-start.5 = (bf16[256,256]{1,0:T(8,128)(2,1)S(1)}, bf16[256,256]{1,0:T(8,128)(2,1)}, u32[]{:S(2)}) copy-start(bf16[256,256]{1,0:T(8,128)(2,1)} %constant.13.clone.inverse_ref) | copy-start | bytes 393220
  1.8 10.4 %collective-permute-start = (bf16[1024,128]{1,0:T(8,128)(2,1)S(1)}, bf16[1024,128]{1,0:T(8,128)(2,1)S(1)}, u32[]{:S(2)}, u32[]{:S(2)}) collective-permute-start(bf16[1024,128]{1,0:T(8,128)(2,1)S(1)} %broadcast_select_fusion), channel_id=1, source_target_pairs={{0,1},{1,0},{2,3},{3,2},{4,5},{5,4},{6,7},{7,6},{8,9},{9,8},{10,11... | collective-permute-start | bytes 786440 | tf_op jit(solution)/shard_map/ppermute | solution.py:189
  4.9 0.8 %copy-start.2 = (f32[64,128]{1,0:T(8,128)S(1)}, f32[64,128]{1,0:T(8,128)}, u32[]{:S(2)}) copy-start(f32[64,128]{1,0:T(8,128)} %own_ref.1) | copy-start | bytes 98308
  5.5 6.7 %collective-permute-start.2 = (f32[64,128]{1,0:T(8,128)S(1)}, f32[64,128]{1,0:T(8,128)S(1)}, u32[]{:S(2)}, u32[]{:S(2)}) collective-permute-start(f32[64,128]{1,0:T(8,128)S(1)} %get-tuple-element.11), channel_id=1, source_target_pairs={{0,1},{1,0},{2,3},{3,2},{4,5},{5,4},{6,7},{7,6},{8,9},{9,8},{10,11... | collective-permute-start | bytes 98312 | tf_op jit(solution)/shard_map/ppermute | solution.py:201
  5.6 9.0 %collective-permute-start.1 = (f32[64,128]{1,0:T(8,128)S(1)}, f32[64,128]{1,0:T(8,128)S(1)}, u32[]{:S(2)}, u32[]{:S(2)}) collective-permute-start(f32[64,128]{1,0:T(8,128)S(1)} %copy-done.2), channel_id=1, source_target_pairs={{0,1},{1,0},{2,3},{3,2},{4,5},{5,4},{6,7},{7,6},{8,9},{9,8},{10,11... | collective-permute-start | bytes 98312 | tf_op jit(solution)/shard_map/ppermute | solution.py:188
  12.8 4.0 %collective-permute-start.3 = (f32[64,128]{1,0:T(8,128)S(1)}, f32[64,128]{1,0:T(8,128)S(1)}, u32[]{:S(2)}, u32[]{:S(2)}) collective-permute-start(f32[64,128]{1,0:T(8,128)S(1)} %shard_map.80), channel_id=1, source_target_pairs={{0,8},{8,0},{16,24},{24,16},{1,9},{9,1},{17,25},{25,17},{2,10},{10... | collective-permute-start | bytes 98312 | tf_op jit(solution)/shard_map/ppermute | solution.py:228
  16.7 2.9 %copy-start.3 = (f32[1024]{0:T(1024)S(1)}, f32[1024]{0:T(1024)}, u32[]{:S(2)}) copy-start(f32[1024]{0:T(1024)} %param.9) | copy-start | bytes 12292
  16.7 5.1 %collective-permute-start.4 = (f32[64,128]{1,0:T(8,128)S(1)}, f32[64,128]{1,0:T(8,128)S(1)}, u32[]{:S(2)}, u32[]{:S(2)}) collective-permute-start(f32[64,128]{1,0:T(8,128)S(1)} %add.6), channel_id=1, source_target_pairs={{0,16},{8,24},{16,0},{24,8},{1,17},{9,25},{17,1},{25,9},{2,18},{10... | collective-permute-start | bytes 98312 | tf_op jit(solution)/shard_map/ppermute | solution.py:228
where the time goes:
time: 22.7 us; the launch traced here: 22.5 us
  starting transfers between devices  9.69 us (43%)
  waiting for transfers between devices  5.23 us (23%)
  Pallas kernels  4.95 us (22%)
  other arithmetic  1.75 us (8%)
  between operations  0.7 us (3%)
    pallas_call x4, Pallas kernels, call(): pl.pallas_call(kernel, out_shape=out_shape, in_specs=[VMEM_SPEC] * len(op...  4.95 us
    ppermute x2, starting transfers between devices, paired(): lax.ppermute(total, 'dp', [(i, i ^ step) for i in range(sequences)])  4.71 us
    ppermute x1, waiting for transfers between devices, paired(): other_taps = lax.ppermute(taps, 'context', swap)  4.7 us
    ppermute x1, starting transfers between devices, paired(): moved = lax.ppermute(jnp.where(first, own_in, own_grad), 'context', swap)  3.03 us
    ppermute x1, starting transfers between devices, paired(): other_filters = lax.ppermute(filters, 'context', swap)  1.88 us
    select_n x1, other arithmetic, paired(): moved = lax.ppermute(jnp.where(first, own_in, own_grad), 'context', swap)  1.13 us
    mul x1, other arithmetic, paired(): return (grad_input[None], total * norm_scale)  0.62 us
    ppermute x2, waiting for transfers between devices, paired(): lax.ppermute(total, 'dp', [(i, i ^ step) for i in range(sequences)])  0.52 us
  transfers between devices with their start and end apart: 5, of which 2 were waited for; matrix products, arithmetic and copies ran while one was open for 0% of the time, Pallas kernels for 22%

commit v1 on v0

--- a/solution.py
+++ b/solution.py
@@ -77,7 +77,7 @@
     return (1 - 2 * (lane % 2)).astype(jnp.float32)
 
 
-def local_lag_kernel(in_ref, grad_ref, forward_ref, inverse_ref, part_ref, lag_ref, taps_ref):
+def local_lag(in_ref, grad_ref, forward_ref, inverse_ref, part_ref, lag_ref, taps_ref):
     first = lax.axis_index("context") == 0
     chans, tok = in_ref.shape
     rows = GROUP * 8
@@ -91,10 +91,83 @@
         lag_ref[groups, :tok] = group_sum(lag_re)
         lag_ref[groups, tok:] = group_sum(lag_im)
         part_ref[span, :] = jnp.where(first, in_spec, grad_spec)
-    taps_ref[...] = inverse_float(lag_ref[...], inverse_ref[...])
-
-
-def cross_lag_kernel(moved_ref, part_ref, lag_ref, taps_ref, forward_ref, inverse_ref, out_ref, sum_ref):
+    taps_ref[...] = jnp.where(first, 0.0, inverse_float(lag_ref[...], inverse_ref[...]))
+
+
+def local_corr(grad_ref, own_ref, skip_ref, forward_ref, inverse_ref, corr_ref, gained_ref, base_ref):
+    first = lax.axis_index("context") == 0
+    chans, tok = grad_ref.shape
+    rows = GROUP * 8
+    forward = forward_ref[...]
+    inverse = inverse_ref[...]
+    base_ref[...] = jnp.where(first, forward_float(own_ref[...], forward), 0.0)
+    for start in range(0, chans, rows):
+        span = pl.ds(start, rows)
+        groups = pl.ds(start // GROUP, rows // GROUP)
+        grad = grad_ref[span, :]
+        spec = forward_exact(grad, forward)
+        prod = conj_mul(group_spread(base_ref[groups, :]), spec)
+        corr_ref[span, :] = inverse_float(jnp.concatenate(prod, axis=1), inverse)
+        gain = jnp.broadcast_to(skip_ref[start // rows, :][None, :], (tok, rows)).T
+        gained_ref[span, :] = gain * grad.astype(jnp.float32)
+
+
+def late_core():
+    return lax.axis_index("tensor") % 2 == 1
+
+
+def before_swap_kernel(*refs):
+    sources, (picked_ref, part_ref, lag_ref, taps_ref, corr_ref, gained_ref) = refs[:6], refs[6:12]
+    base_ref, sems, *held = refs[12:]
+    first = lax.axis_index("context") == 0
+    copies = [pltpu.make_async_copy(*pair, sems.at[i]) for i, pair in enumerate(zip(sources, held))]
+
+    def send(ref):
+        copy = pltpu.make_async_copy(ref, picked_ref, sems.at[len(copies)])
+        copy.start()
+        copy.wait()
+
+    @pl.when(late_core())
+    def _():
+        for batch in (copies[:1], copies[1:]):
+            for copy in batch:
+                copy.start()
+            for copy in batch:
+                copy.wait()
+        in_ref, grad_ref, own_ref, skip_ref, forward_ref, inverse_ref = held
+        picked_ref[...] = jnp.where(first, in_ref[...], grad_ref[...])
+        local_lag(in_ref, grad_ref, forward_ref, inverse_ref, part_ref, lag_ref, taps_ref)
+        local_corr(grad_ref, own_ref, skip_ref, forward_ref, inverse_ref, corr_ref, gained_ref, base_ref)
+
+    @pl.when(jnp.logical_not(late_core()) & first)
+    def _():
+        send(sources[0])
+
+    @pl.when(jnp.logical_not(late_core()) & jnp.logical_not(first))
+    def _():
+        send(sources[1])
+
+
+def lag_after_kernel(in_ref, grad_ref, forward_ref, inverse_ref, *rest):
+    part_ref, lag_ref, taps_ref = rest[3:]
+
+    @pl.when(jnp.logical_not(late_core()))
+    def _():
+        local_lag(in_ref, grad_ref, forward_ref, inverse_ref, part_ref, lag_ref, taps_ref)
+
+
+def corr_after_kernel(grad_ref, own_ref, skip_ref, forward_ref, inverse_ref, *rest):
+    corr_ref, gained_ref, base_ref, held_ref, sem = rest[2:]
+
+    @pl.when(jnp.logical_not(late_core()))
+    def _():
+        copy = pltpu.make_async_copy(skip_ref, held_ref, sem)
+        copy.start()
+        copy.wait()
+        local_corr(grad_ref, own_ref, held_ref, forward_ref, inverse_ref, corr_ref, gained_ref, base_ref)
+
+
+def cross_lag_kernel(moved_ref, part_ref, lag_ref, forward_ref, inverse_ref, out_ref, sum_ref):
     first = lax.axis_index("context") == 0
     chans, tok = moved_ref.shape
     rows = GROUP * 8
@@ -115,55 +188,50 @@
         ],
         axis=1,
     )
-    taps = inverse_float(total, inverse_ref[...])
-    out_ref[...] = taps + jnp.where(first, taps_ref[...], 0.0)
-
-
-def local_corr_kernel(grad_ref, own_ref, other_ref, forward_ref, inverse_ref, corr_ref, turn_ref, base_ref):
+    out_ref[...] = inverse_float(total, inverse_ref[...])
+
+
+def cross_corr_kernel(
+    moved_ref, grad_ref, own_ref, other_ref, corr_ref, gained_ref, forward_ref, inverse_ref, out_ref, turn_ref
+):
     first = lax.axis_index("context") == 0
-    chans, tok = grad_ref.shape
-    rows = GROUP * 8
-    forward = forward_ref[...]
-    inverse = inverse_ref[...]
-    base = forward_float(jnp.where(first, own_ref[...], other_ref[...]), forward)
-    tail = forward_float(jnp.where(first, other_ref[...], own_ref[...]), forward)
-    base_ref[...] = base
-    sign = sign_row(tok)
-    turn_ref[:, :tok] = jnp.where(first, tail[:, :tok] - sign * base[:, tok:], 0.0)
-    turn_ref[:, tok:] = jnp.where(first, tail[:, tok:] + sign * base[:, :tok], 0.0)
-    for start in range(0, chans, rows):
-        span = pl.ds(start, rows)
-        groups = pl.ds(start // GROUP, rows // GROUP)
-        spec = forward_exact(grad_ref[span, :], forward)
-        prod = conj_mul(group_spread(base_ref[groups, :]), spec)
-        corr_ref[span, :] = inverse_float(jnp.concatenate(prod, axis=1), inverse)
-
-
-def cross_corr_kernel(moved_ref, grad_ref, skip_ref, corr_ref, turn_ref, forward_ref, inverse_ref, out_ref):
     chans, tok = moved_ref.shape
     rows = GROUP * 8
     forward = forward_ref[...]
     inverse = inverse_ref[...]
+    own = forward_float(own_ref[...], forward)
+    other = forward_float(other_ref[...], forward)
+    sign = sign_row(tok)
+    turn_ref[:, :tok] = other[:, :tok] - jnp.where(first, sign * own[:, tok:], 0.0)
+    turn_ref[:, tok:] = other[:, tok:] + jnp.where(first, sign * own[:, :tok], 0.0)
     for start in range(0, chans, rows):
         span = pl.ds(start, rows)
-        groups = pl.ds(start // GROUP, rows // GROUP)
-        spec = forward_exact(moved_ref[span, :], forward)
-        prod = conj_mul(group_spread(turn_ref[groups, :]), spec)
-        corr = corr_ref[span, :] + inverse_float(jnp.concatenate(prod, axis=1), inverse)
+        spec = forward_exact(jnp.where(first, moved_ref[span, :], grad_ref[span, :]), forward)
+        turn = group_spread(turn_ref[pl.ds(start // GROUP, rows // GROUP), :])
+        corr = corr_ref[span, :] + inverse_float(jnp.concatenate(conj_mul(turn, spec), axis=1), inverse)
         corr = corr.astype(jnp.bfloat16).astype(jnp.float32)
-        gain = jnp.broadcast_to(skip_ref[start // rows, :][None, :], (tok, rows)).T
-        out_ref[span, :] = (corr + gain * grad_ref[span, :].astype(jnp.float32)).astype(jnp.bfloat16)
+        out_ref[span, :] = (corr + gained_ref[span, :]).astype(jnp.bfloat16)
+
+
+def store_kernel(held_ref, out_ref, sem):
+    copy = pltpu.make_async_copy(held_ref, out_ref, sem)
+    copy.start()
+    copy.wait()
 
 
 VMEM_SPEC = pl.BlockSpec(memory_space=pltpu.VMEM)
 
 
-def call(kernel, out_shape, scratch, cost, *operands):
+ANY_SPEC = pl.BlockSpec(memory_space=pl.ANY)
+
+
+def call(kernel, out_shape, scratch, cost, *operands, in_specs=None, out_specs=None, aliases={}):
     return pl.pallas_call(
         kernel,
         out_shape=out_shape,
-        in_specs=[VMEM_SPEC] * len(operands),
-        out_specs=jax.tree.map(lambda _: VMEM_SPEC, out_shape),
+        in_specs=in_specs or [VMEM_SPEC] * len(operands),
+        input_output_aliases=aliases,
+        out_specs=out_specs or jax.tree.map(lambda _: VMEM_SPEC, out_shape),
         scratch_shapes=scratch,
         cost_estimate=pl.CostEstimate(flops=cost, bytes_accessed=cost // 256, transcendentals=0),
         compiler_params=pltpu.CompilerParams(vmem_limit_bytes=24 * 1024 * 1024),
@@ -178,55 +246,82 @@
     chans, tok = inputs.shape[1:]
     groups = filters.shape[0]
     sequences = lax.axis_size("dp")
-    first = lax.axis_index("context") == 0
     swap = [(0, 1), (1, 0)]
     forward, inverse = block_tables(tok)
     own_in, own_grad = inputs[0], out_grad[0]
     skip_rows = skip.reshape(-1, GROUP * 8)
     cost = 4 * chans * tok * tok
-
-    other_filters = lax.ppermute(filters, "context", swap)
-    moved = lax.ppermute(jnp.where(first, own_in, own_grad), "context", swap)
+    wide = pltpu.VMEM((chans, tok), jnp.float32)
+    spectra = pltpu.VMEM((groups, 2 * tok), jnp.float32)
+
+    work = (own_in, own_grad, filters, skip_rows, forward, inverse)
+    results = (
+        pltpu.VMEM((chans, 2 * tok), jnp.float32),
+        spectra,
+        pltpu.VMEM((groups, tok), jnp.float32),
+        wide,
+        wide,
+    )
+    picked, *held = call(
+        before_swap_kernel,
+        (pltpu.VMEM((chans, tok), jnp.bfloat16),) + results,
+        [spectra, pltpu.SemaphoreType.DMA((len(work) + 1,))] + [pltpu.VMEM(v.shape, v.dtype) for v in work],
+        cost,
+        *(pltpu.with_memory_space_constraint(v, pltpu.HBM) for v in work),
+        in_specs=[ANY_SPEC] * len(work),
+    )
+    moved = lax.ppermute(picked, "context", swap)
     part, lag, taps = call(
-        local_lag_kernel,
-        (
-            pltpu.VMEM((chans, 2 * tok), jnp.float32),
-            pltpu.VMEM((groups, 2 * tok), jnp.float32),
-            pltpu.VMEM((groups, tok), jnp.float32),
-        ),
+        lag_after_kernel,
+        results[:3],
         [],
         8 * cost,
-        own_in, own_grad, forward, inverse,
+        own_in, own_grad, forward, inverse, *map(in_vmem, held[:3]),
+        aliases={4: 0, 5: 1, 6: 2},
     )
     other_taps = lax.ppermute(taps, "context", swap)
-    corr, turn = call(
-        local_corr_kernel,
-        (
-            pltpu.VMEM((chans, tok), jnp.float32),
-            pltpu.VMEM((groups, 2 * tok), jnp.float32),
-        ),
-        [pltpu.VMEM((groups, 2 * tok), jnp.float32)],
+    held = lax.optimization_barrier((part, *held[3:]))
+    part = held[0]
+    corr, gained = call(
+        corr_after_kernel,
+        results[3:],
+        [spectra, pltpu.VMEM(skip_rows.shape, skip.dtype), pltpu.SemaphoreType.DMA],
         8 * cost,
-        own_grad, filters, other_filters, forward, inverse,
-    )
-    total = call(
+        own_grad, filters, pltpu.with_memory_space_constraint(skip_rows, pltpu.HBM), forward, inverse,
+        *map(in_vmem, held[1:]),
+        in_specs=[VMEM_SPEC] * 2 + [ANY_SPEC] + [VMEM_SPEC] * 4,
+        aliases={5: 0, 6: 1},
+    )
+    filters, part, corr = lax.optimization_barrier((filters, part, corr))
+    other_filters = lax.ppermute(filters, "context", swap)
+    total = other_taps + call(
         cross_lag_kernel,
         pltpu.VMEM((groups, tok), jnp.float32),
-        [pltpu.VMEM((groups, 2 * tok), jnp.float32)],
+        [spectra],
         8 * cost,
-        in_vmem(moved), part, lag, other_taps, forward, inverse,
+        in_vmem(moved), part, lag, forward, inverse,
     )
     grad_input = call(
         cross_corr_kernel,
-        jax.ShapeDtypeStruct((chans, tok), jnp.bfloat16),
-        [],
+        pltpu.VMEM((chans, tok), jnp.bfloat16),
+        [spectra],
         8 * cost,
-        in_vmem(moved), own_grad, skip_rows, corr, turn, forward, inverse,
+        in_vmem(moved), own_grad, filters, in_vmem(other_filters), corr, gained, forward, inverse,
     )
     step = 1
     while step < sequences:
         total = total + lax.ppermute(total, "dp", [(i, i ^ step) for i in range(sequences)])
+        total, grad_input = lax.optimization_barrier((total, grad_input))
         step *= 2
+        if 2 * step == sequences:
+            grad_input = call(
+                store_kernel,
+                jax.ShapeDtypeStruct((chans, tok), jnp.bfloat16),
+                [pltpu.SemaphoreType.DMA],
+                cost,
+                in_vmem(grad_input),
+                out_specs=ANY_SPEC,
+            )
     norm_scale = 1.0 / math.sqrt(sequences * GROUP * 2 * tok)
     return (grad_input[None], total * norm_scale)
 

time: 22.7 us -> 20.7 us (0.912)
  the two profiles are of different devices: /device:TPU:0 before, /device:TPU:1 now
where the time goes in v1:
time: 20.7 us; the launch traced here: 20.5 us
  starting transfers between devices  7.37 us (36%)
  Pallas kernels  7.12 us (34%)
  waiting for transfers between devices  3.94 us (19%)
  between operations  0.74 us (4%)
  local copies, waits for them, and re-layouts  0.64 us (3%)
  other arithmetic  0.64 us (3%)
    pallas_call x6, Pallas kernels, call(): pl.pallas_call(kernel, out_shape=out_shape, in_specs=in_specs or [VMEM_SP...  7.12 us
    ppermute x2, starting transfers between devices, paired(): lax.ppermute(total, 'dp', [(i, i ^ step) for i in range(sequences)])  4.24 us
    ppermute x1, waiting for transfers between devices, paired(): moved = lax.ppermute(picked, 'context', swap)  3.31 us
    ppermute x1, starting transfers between devices, paired(): moved = lax.ppermute(picked, 'context', swap)  2.14 us
    ppermute x1, starting transfers between devices, paired(): other_filters = lax.ppermute(filters, 'context', swap)  0.88 us
    unnamed x10, local copies, waits for them, and re-layouts  0.64 us
    ppermute x2, waiting for transfers between devices, paired(): lax.ppermute(total, 'dp', [(i, i ^ step) for i in range(sequences)])  0.63 us
    mul x1, other arithmetic, paired(): return (grad_input[None], total * norm_scale)  0.62 us
  transfers between devices with their start and end apart: 5, of which 2 were waited for; matrix products, arithmetic and copies ran while one was open for 0% of the time, Pallas kernels for 14%

profile of v1, /device:TPU:1, one launch (start us, length us, event | category | flops | bytes accessed | tf_op | source)
XLA Modules:
  0.0 20.5 jit_solution(461732072182738206)
XLA Ops:
  0.6 0.0 copy-start
  0.6 0.0 copy-start.1
  0.7 0.0 copy-start.2
  0.7 0.0 copy-start.3
  0.7 4.2 %shard_map.77 = (bf16[1024,128]{1,0:T(8,128)(2,1)S(1)}, f32[1024,256]{1,0:T(8,128)S(1)}, f32[64,256]{1,0:T(8,128)S(1)}, f32[64,128]{1,0:T(8,128)S(1)}, f32[1024,128]{1,0:T(8,128)S(1)}, /*index=5*/f32[1024,128]{1,0:T(8,128)S(1)}) custom-call(bf16[1024,128]{1,0:T(8,128)(2,1)} %bitcast.8, bf16[1024,128]{1,0:T(8,128)(2,1)} %bitcast.4, f32[64,128]{1,0:T(8,128)} %own_ref.2, ...), custom_call_target="tpu_custom_call" | custom-call | flops 67108864 | bytes 262144 | tf_op jit(solution)/shard_map/pallas_call | solution.py:229
  4.9 2.1 %collective-permute-start.1 = (bf16[1024,128]{1,0:T(8,128)(2,1)S(1)}, bf16[1024,128]{1,0:T(8,128)(2,1)S(1)}, u32[]{:S(2)}, u32[]{:S(2)}) collective-permute-start(bf16[1024,128]{1,0:T(8,128)(2,1)S(1)} %get-tuple-element.27), channel_id=1, source_target_pairs={{0,1},{1,0},{2,3},{3,2},{4,5},{5,4},{6,7},{7,6},{8,9},{9,8},{10,11... | collective-permute-start | bytes 786440 | tf_op jit(solution)/shard_map/ppermute | solution.py:273
  7.1 0.0 copy-done
  7.1 0.0 copy-done.1
  7.1 0.0 copy-done.2
  7.1 0.0 copy-done.3
  7.1 0.0 copy-start.4
  7.1 0.1 collective-permute-start
  7.2 0.6 %copy-done.4 = f32[64,128]{1,0:T(8,128)S(1)} copy-done((f32[64,128]{1,0:T(8,128)S(1)}, f32[64,128]{1,0:T(8,128)}, u32[]{:S(2)}) %copy-start.4) | copy-done | bytes 32792
  7.9 0.9 %collective-permute-start.3 = (f32[64,128]{1,0:T(8,128)S(1)}, f32[64,128]{1,0:T(8,128)S(1)}, u32[]{:S(2)}, u32[]{:S(2)}) collective-permute-start(f32[64,128]{1,0:T(8,128)S(1)} %copy-done.4), channel_id=1, source_target_pairs={{0,1},{1,0},{2,3},{3,2},{4,5},{5,4},{6,7},{7,6},{8,9},{9,8},{10,11... | collective-permute-start | bytes 98312 | tf_op jit(solution)/shard_map/ppermute | solution.py:296
  8.7 3.3 %collective-permute-done.1.moved_ref = bf16[1024,128]{1,0:T(8,128)(2,1)S(1)} collective-permute-done((bf16[1024,128]{1,0:T(8,128)(2,1)S(1)}, bf16[1024,128]{1,0:T(8,128)(2,1)S(1)}, u32[]{:S(2)}, u32[]{:S(2)}) %collective-permute-start.1) | collective-permute-done | bytes 262176 | tf_op jit(solution)/shard_map/ppermute | solution.py:273
  12.0 0.5 %shard_map.80 = f32[64,128]{1,0:T(8,128)S(1)} custom-call(bf16[1024,128]{1,0:T(8,128)(2,1)S(1)} %collective-permute-done.1.moved_ref, f32[1024,256]{1,0:T(8,128)S(1)} %get-tuple-element.35.part_ref, f32[64,256]{1,0:T(8,128)S(1)} %get-tuple-element.36.lag_ref, bf16[256,256]{1,0:T(8,128)(2,1)S(1)} %copy-done.2, bf16[256,256]{1,0:T(8,128)(2,1)S(1)} %copy-done.1), custom_call_target="tpu_custom_call" | custom-call | flops 536870912 | bytes 2097152 | tf_op jit(solution)/shard_map/pallas_call | solution.py:229
  12.6 0.0 collective-permute-done
  12.6 1.9 %collective-permute-start.2 = (f32[64,128]{1,0:T(8,128)S(1)}, f32[64,128]{1,0:T(8,128)S(1)}, u32[]{:S(2)}, u32[]{:S(2)}) collective-permute-start(f32[64,128]{1,0:T(8,128)S(1)} %add.9), channel_id=1, source_target_pairs={{0,8},{8,0},{16,24},{24,16},{1,9},{9,1},{17,25},{25,17},{2,10},{10... | collective-permute-start | bytes 98312 | tf_op jit(solution)/shard_map/ppermute | solution.py:313
  14.5 0.0 collective-permute-done.3.other_ref
  14.5 1.6 %shard_map.81.held_ref = bf16[1024,128]{1,0:T(8,128)(2,1)S(1)} custom-call(bf16[1024,128]{1,0:T(8,128)(2,1)S(1)} %collective-permute-done.1.moved_ref, bf16[1024,128]{1,0:T(8,128)(2,1)S(1)} %bitcast.7, f32[64,128]{1,0:T(8,128)S(1)} %copy-done.4, f32[64,128]{1,0:T(8,128)S(1)} %collective-permute-done.3.other_ref, f32[1024,128]{1,0:T(8,128)S(1)} %get-tuple-element.38.corr_ref, ...), custom_call_target="tpu_custom_call" | custom-call | flops 536870912 | bytes 2097152 | tf_op jit(solution)/shard_map/pallas_call | solution.py:229
  16.1 0.0 collective-permute-done.2
  16.1 2.4 %collective-permute-start.4 = (f32[64,128]{1,0:T(8,128)S(1)}, f32[64,128]{1,0:T(8,128)S(1)}, u32[]{:S(2)}, u32[]{:S(2)}) collective-permute-start(f32[64,128]{1,0:T(8,128)S(1)} %add.10), channel_id=1, source_target_pairs={{0,16},{8,24},{16,0},{24,8},{1,17},{9,25},{17,1},{25,9},{2,18},{10... | collective-permute-start | bytes 98312 | tf_op jit(solution)/shard_map/ppermute | solution.py:313
  18.5 0.7 %shard_map.82 = bf16[1024,128]{1,0:T(8,128)(2,1)} custom-call(bf16[1024,128]{1,0:T(8,128)(2,1)S(1)} %shard_map.81.held_ref), custom_call_target="tpu_custom_call" | custom-call | flops 67108864 | bytes 262144 | tf_op jit(solution)/shard_map/pallas_call | solution.py:229
  19.2 0.6 %collective-permute-done.4 = f32[64,128]{1,0:T(8,128)S(1)} collective-permute-done((f32[64,128]{1,0:T(8,128)S(1)}, f32[64,128]{1,0:T(8,128)S(1)}, u32[]{:S(2)}, u32[]{:S(2)}) %collective-permute-start.4) | collective-permute-done | bytes 32800 | tf_op jit(solution)/shard_map/ppermute | solution.py:313
  19.8 0.6 %broadcast_multiply_fusion = f32[64,128]{1,0:T(8,128)} fusion(f32[64,128]{1,0:T(8,128)S(1)} %add.11), kind=kLoop, calls=%fused_computation | loop fusion | flops 8192 | bytes 65536 | tf_op jit(solution)/shard_map/mul | solution.py:326
  (5 shorter events, 0.1 us)
Async XLA Ops:
  0.6 6.4 %copy-start = (bf16[1,1024,128]{2,1,0:T(8,128)(2,1)S(1)}, bf16[1,1024,128]{2,1,0:T(8,128)(2,1)}, u32[]{:S(2)}) copy-start(bf16[1,1024,128]{2,1,0:T(8,128)(2,1)} %param.7) | copy-start | bytes 786436
  0.6 6.4 %copy-start.1 = (bf16[256,256]{1,0:T(8,128)(2,1)S(1)}, bf16[256,256]{1,0:T(8,128)(2,1)}, u32[]{:S(2)}) copy-start(bf16[256,256]{1,0:T(8,128)(2,1)} %constant.7.clone.refs_5_.inverse_ref) | copy-start | bytes 393220
  0.7 6.4 %copy-start.2 = (bf16[256,256]{1,0:T(8,128)(2,1)S(1)}, bf16[256,256]{1,0:T(8,128)(2,1)}, u32[]{:S(2)}) copy-start(bf16[256,256]{1,0:T(8,128)(2,1)} %constant.6.clone.refs_4_.forward_ref) | copy-start | bytes 393220
  0.7 6.4 %copy-start.3 = (bf16[1,1024,128]{2,1,0:T(8,128)(2,1)S(1)}, bf16[1,1024,128]{2,1,0:T(8,128)(2,1)}, u32[]{:S(2)}) copy-start(bf16[1,1024,128]{2,1,0:T(8,128)(2,1)} %param.6) | copy-start | bytes 786436
  4.9 7.1 %collective-permute-start.1 = (bf16[1024,128]{1,0:T(8,128)(2,1)S(1)}, bf16[1024,128]{1,0:T(8,128)(2,1)S(1)}, u32[]{:S(2)}, u32[]{:S(2)}) collective-permute-start(bf16[1024,128]{1,0:T(8,128)(2,1)S(1)} %get-tuple-element.27), channel_id=1, source_target_pairs={{0,1},{1,0},{2,3},{3,2},{4,5},{5,4},{6,7},{7,6},{8,9},{9,8},{10,11... | collective-permute-start | bytes 786440 | tf_op jit(solution)/shard_map/ppermute | solution.py:273
  7.1 0.8 %copy-start.4 = (f32[64,128]{1,0:T(8,128)S(1)}, f32[64,128]{1,0:T(8,128)}, u32[]{:S(2)}) copy-start(f32[64,128]{1,0:T(8,128)} %own_ref.2) | copy-start | bytes 98308
  7.1 5.5 %collective-permute-start = (f32[64,128]{1,0:T(8,128)S(1)}, f32[64,128]{1,0:T(8,128)S(1)}, u32[]{:S(2)}, u32[]{:S(2)}) collective-permute-start(f32[64,128]{1,0:T(8,128)S(1)} %get-tuple-element.26), channel_id=1, source_target_pairs={{0,1},{1,0},{2,3},{3,2},{4,5},{5,4},{6,7},{7,6},{8,9},{9,8},{10,11... | collective-permute-start | bytes 98312 | tf_op jit(solution)/shard_map/ppermute | solution.py:282
  7.9 6.6 %collective-permute-start.3 = (f32[64,128]{1,0:T(8,128)S(1)}, f32[64,128]{1,0:T(8,128)S(1)}, u32[]{:S(2)}, u32[]{:S(2)}) collective-permute-start(f32[64,128]{1,0:T(8,128)S(1)} %copy-done.4), channel_id=1, source_target_pairs={{0,1},{1,0},{2,3},{3,2},{4,5},{5,4},{6,7},{7,6},{8,9},{9,8},{10,11... | collective-permute-start | bytes 98312 | tf_op jit(solution)/shard_map/ppermute | solution.py:296
  12.6 3.5 %collective-permute-start.2 = (f32[64,128]{1,0:T(8,128)S(1)}, f32[64,128]{1,0:T(8,128)S(1)}, u32[]{:S(2)}, u32[]{:S(2)}) collective-permute-start(f32[64,128]{1,0:T(8,128)S(1)} %add.9), channel_id=1, source_target_pairs={{0,8},{8,0},{16,24},{24,16},{1,9},{9,1},{17,25},{25,17},{2,10},{10... | collective-permute-start | bytes 98312 | tf_op jit(solution)/shard_map/ppermute | solution.py:313
  16.1 3.7 %collective-permute-start.4 = (f32[64,128]{1,0:T(8,128)S(1)}, f32[64,128]{1,0:T(8,128)S(1)}, u32[]{:S(2)}, u32[]{:S(2)}) collective-permute-start(f32[64,128]{1,0:T(8,128)S(1)} %add.10), channel_id=1, source_target_pairs={{0,16},{8,24},{16,0},{24,8},{1,17},{9,25},{17,1},{25,9},{2,18},{10... | collective-permute-start | bytes 98312 | tf_op jit(solution)/shard_map/ppermute | solution.py:313

commit v2 on v0

--- a/solution.py
+++ b/solution.py
@@ -1,3 +1,4 @@
+import functools
 import math
 
 import jax
@@ -27,6 +28,10 @@
     return pair
 
 
+def block_rows(chans):
+    return math.gcd(chans // 2, GROUP * 32)
+
+
 def matmul(left, right):
     return jnp.dot(left, right, preferred_element_type=jnp.float32)
 
@@ -77,10 +82,10 @@
     return (1 - 2 * (lane % 2)).astype(jnp.float32)
 
 
-def local_lag_kernel(in_ref, grad_ref, forward_ref, inverse_ref, part_ref, lag_ref, taps_ref):
+def local_lag(in_ref, grad_ref, forward_ref, inverse_ref, part_ref, lag_ref, taps_ref):
     first = lax.axis_index("context") == 0
     chans, tok = in_ref.shape
-    rows = GROUP * 8
+    rows = block_rows(chans)
     forward = forward_ref[...]
     for start in range(0, chans, rows):
         span = pl.ds(start, rows)
@@ -91,18 +96,61 @@
         lag_ref[groups, :tok] = group_sum(lag_re)
         lag_ref[groups, tok:] = group_sum(lag_im)
         part_ref[span, :] = jnp.where(first, in_spec, grad_spec)
-    taps_ref[...] = inverse_float(lag_ref[...], inverse_ref[...])
-
-
-def cross_lag_kernel(moved_ref, part_ref, lag_ref, taps_ref, forward_ref, inverse_ref, out_ref, sum_ref):
+    taps_ref[...] = jnp.where(first, 0.0, inverse_float(lag_ref[...], inverse_ref[...]))
+
+
+def local_corr(grad_ref, own_ref, skip_ref, forward_ref, inverse_ref, corr_ref, gained_ref, base_ref):
     first = lax.axis_index("context") == 0
-    chans, tok = moved_ref.shape
-    rows = GROUP * 8
+    chans, tok = grad_ref.shape
+    rows = block_rows(chans)
+    forward = forward_ref[...]
+    inverse = inverse_ref[...]
+    base_ref[...] = jnp.where(first, forward_float(own_ref[...], forward), 0.0)
+    for start in range(0, chans, rows):
+        span = pl.ds(start, rows)
+        groups = pl.ds(start // GROUP, rows // GROUP)
+        grad = grad_ref[span, :]
+        spec = forward_exact(grad, forward)
+        prod = conj_mul(group_spread(base_ref[groups, :]), spec)
+        corr_ref[span, :] = inverse_float(jnp.concatenate(prod, axis=1), inverse)
+        for at in range(0, rows, tok):
+            gain = jnp.broadcast_to(skip_ref[(start + at) // tok, :][None, :], (tok, tok)).T
+            gained_ref[pl.ds(start + at, tok), :] = gain * grad[at : at + tok, :].astype(jnp.float32)
+
+
+def load_kernel(in_ref, grad_ref, filters_ref, skip_ref, *refs):
+    first = lax.axis_index("context") == 0
+    *parts, in_held, grad_held, filters_held, skip_held, sems = refs
+    pairs = ((in_ref, in_held), (grad_ref, grad_held), (filters_ref, filters_held), (skip_ref, skip_held))
+    copies = [pltpu.make_async_copy(*pair, sems.at[i]) for i, pair in enumerate(pairs)]
+    for copy in copies:
+        copy.start()
+    for copy in copies:
+        copy.wait()
+    start = 0
+    for part in parts:
+        span = pl.ds(start, part.shape[0])
+        part[...] = jnp.where(first, in_held[span, :], grad_held[span, :])
+        start += part.shape[0]
+
+
+def moved_block(parts, start, rows):
+    for part in parts:
+        if start < part.shape[0]:
+            return part[pl.ds(start, rows), :]
+        start -= part.shape[0]
+
+
+def cross_lag_kernel(*refs):
+    *parts, part_ref, lag_ref, forward_ref, inverse_ref, out_ref, sum_ref = refs
+    first = lax.axis_index("context") == 0
+    chans, tok = part_ref.shape[0], out_ref.shape[1]
+    rows = block_rows(chans)
     forward = forward_ref[...]
     for start in range(0, chans, rows):
         span = pl.ds(start, rows)
         groups = pl.ds(start // GROUP, rows // GROUP)
-        spec = forward_exact(moved_ref[span, :], forward)
+        spec = forward_exact(moved_block(parts, start, rows), forward)
         re, im = conj_mul(part_ref[span, :], spec)
         sum_ref[groups, :tok] = group_sum(re)
         sum_ref[groups, tok:] = group_sum(im)
@@ -115,55 +163,53 @@
         ],
         axis=1,
     )
-    taps = inverse_float(total, inverse_ref[...])
-    out_ref[...] = taps + jnp.where(first, taps_ref[...], 0.0)
-
-
-def local_corr_kernel(grad_ref, own_ref, other_ref, forward_ref, inverse_ref, corr_ref, turn_ref, base_ref):
+    out_ref[...] = inverse_float(total, inverse_ref[...])
+
+
+def cross_corr_kernel(*refs):
+    *parts, grad_ref, own_ref, other_ref, corr_ref, gained_ref, forward_ref, inverse_ref, out_ref, turn_ref = refs
     first = lax.axis_index("context") == 0
     chans, tok = grad_ref.shape
-    rows = GROUP * 8
+    rows = block_rows(chans)
     forward = forward_ref[...]
     inverse = inverse_ref[...]
-    base = forward_float(jnp.where(first, own_ref[...], other_ref[...]), forward)
-    tail = forward_float(jnp.where(first, other_ref[...], own_ref[...]), forward)
-    base_ref[...] = base
+    own = forward_float(own_ref[...], forward)
+    other = forward_float(other_ref[...], forward)
     sign = sign_row(tok)
-    turn_ref[:, :tok] = jnp.where(first, tail[:, :tok] - sign * base[:, tok:], 0.0)
-    turn_ref[:, tok:] = jnp.where(first, tail[:, tok:] + sign * base[:, :tok], 0.0)
+    turn_ref[:, :tok] = other[:, :tok] - jnp.where(first, sign * own[:, tok:], 0.0)
+    turn_ref[:, tok:] = other[:, tok:] + jnp.where(first, sign * own[:, :tok], 0.0)
     for start in range(0, chans, rows):
         span = pl.ds(start, rows)
-        groups = pl.ds(start // GROUP, rows // GROUP)
-        spec = forward_exact(grad_ref[span, :], forward)
-        prod = conj_mul(group_spread(base_ref[groups, :]), spec)
-        corr_ref[span, :] = inverse_float(jnp.concatenate(prod, axis=1), inverse)
-
-
-def cross_corr_kernel(moved_ref, grad_ref, skip_ref, corr_ref, turn_ref, forward_ref, inverse_ref, out_ref):
-    chans, tok = moved_ref.shape
-    rows = GROUP * 8
-    forward = forward_ref[...]
-    inverse = inverse_ref[...]
-    for start in range(0, chans, rows):
-        span = pl.ds(start, rows)
-        groups = pl.ds(start // GROUP, rows // GROUP)
-        spec = forward_exact(moved_ref[span, :], forward)
-        prod = conj_mul(group_spread(turn_ref[groups, :]), spec)
-        corr = corr_ref[span, :] + inverse_float(jnp.concatenate(prod, axis=1), inverse)
+        spec = forward_exact(jnp.where(first, moved_block(parts, start, rows), grad_ref[span, :]), forward)
+        turn = group_spread(turn_ref[pl.ds(start // GROUP, rows // GROUP), :])
+        corr = corr_ref[span, :] + inverse_float(jnp.concatenate(conj_mul(turn, spec), axis=1), inverse)
         corr = corr.astype(jnp.bfloat16).astype(jnp.float32)
-        gain = jnp.broadcast_to(skip_ref[start // rows, :][None, :], (tok, rows)).T
-        out_ref[span, :] = (corr + gain * grad_ref[span, :].astype(jnp.float32)).astype(jnp.bfloat16)
+        out_ref[span, :] = (corr + gained_ref[span, :]).astype(jnp.bfloat16)
+
+
+def finish_kernel(scale, left_ref, right_ref, out_ref):
+    out_ref[...] = (left_ref[...] + right_ref[...]) * scale
+
+
+def store_kernel(held_ref, out_ref, sem):
+    copy = pltpu.make_async_copy(held_ref, out_ref, sem)
+    copy.start()
+    copy.wait()
 
 
 VMEM_SPEC = pl.BlockSpec(memory_space=pltpu.VMEM)
 
 
-def call(kernel, out_shape, scratch, cost, *operands):
+ANY_SPEC = pl.BlockSpec(memory_space=pl.ANY)
+
+
+def call(kernel, out_shape, scratch, cost, *operands, in_specs=None, out_specs=None, aliases={}):
     return pl.pallas_call(
         kernel,
         out_shape=out_shape,
-        in_specs=[VMEM_SPEC] * len(operands),
-        out_specs=jax.tree.map(lambda _: VMEM_SPEC, out_shape),
+        in_specs=in_specs or [VMEM_SPEC] * len(operands),
+        input_output_aliases=aliases,
+        out_specs=out_specs or jax.tree.map(lambda _: VMEM_SPEC, out_shape),
         scratch_shapes=scratch,
         cost_estimate=pl.CostEstimate(flops=cost, bytes_accessed=cost // 256, transcendentals=0),
         compiler_params=pltpu.CompilerParams(vmem_limit_bytes=24 * 1024 * 1024),
@@ -174,61 +220,103 @@
     return pltpu.with_memory_space_constraint(value, pltpu.VMEM)
 
 
-def paired(inputs, out_grad, filters, skip):
+def paired(late, inputs, out_grad, filters, skip):
     chans, tok = inputs.shape[1:]
     groups = filters.shape[0]
     sequences = lax.axis_size("dp")
-    first = lax.axis_index("context") == 0
     swap = [(0, 1), (1, 0)]
     forward, inverse = block_tables(tok)
     own_in, own_grad = inputs[0], out_grad[0]
-    skip_rows = skip.reshape(-1, GROUP * 8)
+    skip_rows = skip.reshape(-1, tok)
     cost = 4 * chans * tok * tok
-
-    other_filters = lax.ppermute(filters, "context", swap)
-    moved = lax.ppermute(jnp.where(first, own_in, own_grad), "context", swap)
+    wide = pltpu.VMEM((chans, tok), jnp.float32)
+    spectra = pltpu.VMEM((groups, 2 * tok), jnp.float32)
+
+    rows = block_rows(chans)
+    cut = chans // (2 * rows) * rows
+    block = pltpu.VMEM((chans, tok), jnp.bfloat16)
+    narrow = pltpu.VMEM((groups, tok), jnp.float32)
+    sizes = (cut, chans - cut) if late else (chans,)
+    parts = tuple(pltpu.VMEM((size, tok), jnp.bfloat16) for size in sizes)
+    loaded = call(
+        load_kernel,
+        parts + (block, block, narrow, pltpu.VMEM(skip_rows.shape, jnp.float32)),
+        [pltpu.SemaphoreType.DMA((4,))],
+        cost,
+        *(pltpu.with_memory_space_constraint(v, pltpu.HBM) for v in (own_in, own_grad, filters, skip_rows)),
+        in_specs=[ANY_SPEC] * 4,
+    )
+    own_in, own_grad, own, skip_held = loaded[-4:]
+    moved = [lax.ppermute(loaded[0], "context", swap)]
     part, lag, taps = call(
-        local_lag_kernel,
-        (
-            pltpu.VMEM((chans, 2 * tok), jnp.float32),
-            pltpu.VMEM((groups, 2 * tok), jnp.float32),
-            pltpu.VMEM((groups, tok), jnp.float32),
-        ),
+        local_lag,
+        (pltpu.VMEM((chans, 2 * tok), jnp.float32), spectra, narrow),
         [],
         8 * cost,
         own_in, own_grad, forward, inverse,
     )
+
+    def correlate_local(grad):
+        return call(local_corr, (wide, wide), [spectra], 8 * cost, grad, own, skip_held, forward, inverse)
+
+    if late:
+        corr, gained = correlate_local(own_grad)
+        moved[0], rest, taps, part, own = lax.optimization_barrier((moved[0], loaded[1], taps, part, own, corr))[:5]
+        moved.append(lax.ppermute(rest, "context", swap))
+        taps, own = lax.optimization_barrier((taps, own))
     other_taps = lax.ppermute(taps, "context", swap)
-    corr, turn = call(
-        local_corr_kernel,
-        (
-            pltpu.VMEM((chans, tok), jnp.float32),
-            pltpu.VMEM((groups, 2 * tok), jnp.float32),
-        ),
-        [pltpu.VMEM((groups, 2 * tok), jnp.float32)],
+    if not late:
+        corr, gained = correlate_local(own_grad)
+        own, part, corr = lax.optimization_barrier((own, part, corr))
+    other_filters = lax.ppermute(own, "context", swap)
+    total = other_taps + call(
+        cross_lag_kernel,
+        narrow,
+        [spectra],
         8 * cost,
-        own_grad, filters, other_filters, forward, inverse,
-    )
-    total = call(
-        cross_lag_kernel,
-        pltpu.VMEM((groups, tok), jnp.float32),
-        [pltpu.VMEM((groups, 2 * tok), jnp.float32)],
-        8 * cost,
-        in_vmem(moved), part, lag, other_taps, forward, inverse,
-    )
-    grad_input = call(
-        cross_corr_kernel,
+        *map(in_vmem, moved), part, lag, forward, inverse,
+    )
+
+    def correlate(filters):
+        return call(
+            cross_corr_kernel,
+            pltpu.VMEM((chans, tok), jnp.bfloat16),
+            [spectra],
+            8 * cost,
+            *map(in_vmem, moved), own_grad, own, in_vmem(filters), corr, gained, forward, inverse,
+        )
+
+    norm_scale = 1.0 / math.sqrt(sequences * GROUP * 2 * tok)
+    got, step = jnp.zeros_like(total), 1
+    grad_input = correlate(other_filters) if late else None
+    while step < sequences:
+        got = lax.ppermute(total, "dp", [(i, i ^ step) for i in range(sequences)])
+        step *= 2
+        if step < sequences:
+            if late:
+                got, grad_input = lax.optimization_barrier((got, grad_input))
+            else:
+                got, corr = lax.optimization_barrier((got, corr))
+            total = total + got
+    if not late:
+        grad_input = correlate(other_filters)
+    stored = call(
+        store_kernel,
         jax.ShapeDtypeStruct((chans, tok), jnp.bfloat16),
+        [pltpu.SemaphoreType.DMA],
+        cost,
+        in_vmem(grad_input),
+        out_specs=ANY_SPEC,
+    )
+    got, _ = lax.optimization_barrier((got, stored))
+    grad_filter = call(
+        functools.partial(finish_kernel, norm_scale),
+        jax.ShapeDtypeStruct((groups, tok), jnp.float32),
         [],
-        8 * cost,
-        in_vmem(moved), own_grad, skip_rows, corr, turn, forward, inverse,
-    )
-    step = 1
-    while step < sequences:
-        total = total + lax.ppermute(total, "dp", [(i, i ^ step) for i in range(sequences)])
-        step *= 2
-    norm_scale = 1.0 / math.sqrt(sequences * GROUP * 2 * tok)
-    return (grad_input[None], total * norm_scale)
+        cost,
+        total, got,
+    )
+    return (stored[None], grad_filter)
 
 
 def dft_tables(size_one, size_two):
@@ -364,8 +452,11 @@
 def per_device(inputs, out_grad, filters, skip):
     sequences = lax.axis_size("dp")
     halves = lax.axis_size("context") == 2 and inputs.shape[0] == 1
-    if halves and sequences & (sequences - 1) == 0 and inputs.shape[1] % (GROUP * 8) == 0:
-        return paired(inputs, out_grad, filters, skip)
+    if halves and sequences & (sequences - 1) == 0 and inputs.shape[1] % (2 * inputs.shape[2]) == 0:
+        late = lax.axis_index("tensor") % 2 == 1
+        return lax.cond(
+            late, functools.partial(paired, True), functools.partial(paired, False), inputs, out_grad, filters, skip
+        )
     return owned(inputs, out_grad, filters, skip)
 
 

time: 22.7 us -> 19.9 us (0.88)
  other arithmetic: 1.75 us -> 0.01 us
  waiting for transfers between devices: 5.23 us -> 4.64 us
  starting transfers between devices: 9.69 us -> 9.28 us
    ppermute x1, waiting for transfers between devices: 4.7 us -> 0.01 us  [paired(): other_taps = lax.ppermute(taps, 'context', swap)]
    ppermute x4, waiting for transfers between devices: 0.53 us -> 4.64 us  [the longest x1 3.53 us: paired(): moved = [lax.ppermute(loaded[0], 'context', swap)]]
    select_n x1 -> x0, other arithmetic: 1.13 us -> none  [paired(): moved = lax.ppermute(jnp.where(first, own_in, own_grad), 'context', swap)]
    mul x1 -> x0, other arithmetic: 0.62 us -> none  [paired(): return (grad_input[None], total * norm_scale)]
    ppermute x4, starting transfers between devices: 9.63 us -> 9.23 us  [the longest x2 4.67 us: paired(): got = lax.ppermute(total, 'dp', [(i, i ^ step) for i in range(sequences)])]
    pallas_call x4 -> x7, Pallas kernels: 4.95 us -> 5.13 us  [call(): pl.pallas_call(kernel, out_shape=out_shape, in_specs=in_specs or [VMEM_SP...]
  transfers between devices with their start and end apart: 5 -> 5, of which waited for: 2 -> 3; matrix products, arithmetic and copies ran while one was open for 0% -> 0% of each run, Pallas kernels for 22% -> 17%
where the time goes in v2:
time: 19.9 us; the launch traced here: 19.8 us
  starting transfers between devices  9.28 us (47%)
  Pallas kernels  5.13 us (26%)
  waiting for transfers between devices  4.64 us (23%)
  between operations  0.64 us (3%)
    pallas_call x7, Pallas kernels, call(): pl.pallas_call(kernel, out_shape=out_shape, in_specs=in_specs or [VMEM_SP...  5.13 us
    ppermute x2, starting transfers between devices, paired(): got = lax.ppermute(total, 'dp', [(i, i ^ step) for i in range(sequences)])  4.67 us
    ppermute x1, waiting for transfers between devices, paired(): moved = [lax.ppermute(loaded[0], 'context', swap)]  3.53 us
    ppermute x1, starting transfers between devices, paired(): moved = [lax.ppermute(loaded[0], 'context', swap)]  3.03 us
    ppermute x1, starting transfers between devices, paired(): other_filters = lax.ppermute(own, 'context', swap)  1.52 us
    ppermute x2, waiting for transfers between devices, paired(): got = lax.ppermute(total, 'dp', [(i, i ^ step) for i in range(sequences)])  1.11 us
  transfers between devices with their start and end apart: 5, of which 3 were waited for; matrix products, arithmetic and copies ran while one was open for 0% of the time, Pallas kernels for 17%

profile of v2, /device:TPU:0, one launch (start us, length us, event | category | flops | bytes accessed | tf_op | source)
XLA Modules:
  0.0 19.8 jit_solution(18088991340978386218)
XLA Ops:
  0.6 19.1 %conditional.1 = (bf16[1,1024,128]{2,1,0:T(8,128)(2,1)}, f32[64,128]{1,0:T(8,128)}) conditional(s32[]{:T(128)} %convert_element_type.3, (bf16[1,1024,128]{2,1,0:T(8,128)(2,1)}, bf16[1,1024,128]{2,1,0:T(8,128)(2,1)}, f32[1024]{0:T(1024)}, f32[64,128]{1,0:T(8,128)}, bf16[256,256]{1,0:T(8,128)(2,1)}, /*index=5*/bf16[256,256]{1,0:T(8,128)(2,1)}) %tuple.22, ...), branch_computations={%region_0.1_spmd, %region_1.2_spmd} | conditional | flops 2348826624 | bytes 11993400 | solution.py:457
  0.7 0.0 copy-start
  0.7 0.0 copy-start.2
  0.7 1.2 %branch_0_fun.7 = (bf16[1024,128]{1,0:T(8,128)(2,1)S(1)}, bf16[1024,128]{1,0:T(8,128)(2,1)S(1)}, bf16[1024,128]{1,0:T(8,128)(2,1)S(1)}, f32[64,128]{1,0:T(8,128)S(1)}, f32[8,128]{1,0:T(8,128)S(1)}) custom-call(bf16[1024,128]{1,0:T(8,128)(2,1)} %bitcast.8, bf16[1024,128]{1,0:T(8,128)(2,1)} %bitcast.10, f32[64,128]{1,0:T(8,128)} %get-tuple-element.26.filters_ref, ...), custom_call_target="tpu_custom_call" | custom-call | flops 67108864 | bytes 262144 | tf_op jit(solution)/shard_map/cond/branch_0_fun/pallas_call | solution.py:207
  1.9 3.0 %collective-permute-start = (bf16[1024,128]{1,0:T(8,128)(2,1)S(1)}, bf16[1024,128]{1,0:T(8,128)(2,1)S(1)}, u32[]{:S(2)}, u32[]{:S(2)}) collective-permute-start(bf16[1024,128]{1,0:T(8,128)(2,1)S(1)} %get-tuple-element.28), channel_id=1, source_target_pairs={{0,1},{1,0},{2,3},{3,2},{4,5},{5,4},{6,7},{7,6},{8,9},{9,8},{10,11... | collective-permute-start | bytes 786440 | tf_op jit(solution)/shard_map/cond/branch_0_fun/ppermute | solution.py:250
  4.9 0.0 copy-done
  4.9 0.0 copy-done.2
  4.9 0.6 %branch_0_fun.8 = (f32[1024,256]{1,0:T(8,128)S(1)}, f32[64,256]{1,0:T(8,128)S(1)}, f32[64,128]{1,0:T(8,128)S(1)}) custom-call(bf16[1024,128]{1,0:T(8,128)(2,1)S(1)} %get-tuple-element.31.in_ref, bf16[1024,128]{1,0:T(8,128)(2,1)S(1)} %get-tuple-element.29.grad_ref.refs_1_, bf16[256,256]{1,0:T(8,128)(2,1)S(1)} %copy-done, bf16[256,256]{1,0:T(8,128)(2,1)S(1)} %copy-done.2), custom_call_target="tpu_custom_call" | custom-call | flops 536870912 | bytes 2097152 | tf_op jit(solution)/shard_map/cond/branch_0_fun/pallas_call | solution.py:207
  5.5 0.1 collective-permute-start.2
  5.5 0.8 %branch_0_fun.9 = (f32[1024,128]{1,0:T(8,128)S(1)}, f32[1024,128]{1,0:T(8,128)S(1)}) custom-call(bf16[1024,128]{1,0:T(8,128)(2,1)S(1)} %get-tuple-element.29.grad_ref.refs_1_, f32[64,128]{1,0:T(8,128)S(1)} %get-tuple-element.37.own_ref.refs_2_, f32[8,128]{1,0:T(8,128)S(1)} %get-tuple-element.35.skip_ref, bf16[256,256]{1,0:T(8,128)(2,1)S(1)} %copy-done, ...), custom_call_target="tpu_custom_call" | custom-call | flops 536870912 | bytes 2097152 | tf_op jit(solution)/shard_map/cond/branch_0_fun/pallas_call | solution.py:207
  6.3 3.5 %collective-permute-done.refs_0_ = bf16[1024,128]{1,0:T(8,128)(2,1)S(1)} collective-permute-done((bf16[1024,128]{1,0:T(8,128)(2,1)S(1)}, bf16[1024,128]{1,0:T(8,128)(2,1)S(1)}, u32[]{:S(2)}, u32[]{:S(2)}) %collective-permute-start) | collective-permute-done | bytes 262176 | tf_op jit(solution)/shard_map/cond/branch_0_fun/ppermute | solution.py:250
  9.8 0.5 %branch_0_fun.10 = f32[64,128]{1,0:T(8,128)S(1)} custom-call(bf16[1024,128]{1,0:T(8,128)(2,1)S(1)} %collective-permute-done.refs_0_, f32[1024,256]{1,0:T(8,128)S(1)} %get-tuple-element.39.refs_1_, f32[64,256]{1,0:T(8,128)S(1)} %get-tuple-element.40.refs_2_, bf16[256,256]{1,0:T(8,128)(2,1)S(1)} %copy-done, bf16[256,256]{1,0:T(8,128)(2,1)S(1)} %copy-done.2), custom_call_target="tpu_custom_call" | custom-call | flops 536870912 | bytes 2097152 | tf_op jit(solution)/shard_map/cond/branch_0_fun/pallas_call | solution.py:207
  10.3 0.0 collective-permute-done.2
  10.4 1.9 %collective-permute-start.3 = (f32[64,128]{1,0:T(8,128)S(1)}, f32[64,128]{1,0:T(8,128)S(1)}, u32[]{:S(2)}, u32[]{:S(2)}) collective-permute-start(f32[64,128]{1,0:T(8,128)S(1)} %add.11), channel_id=1, source_target_pairs={{0,8},{8,0},{16,24},{24,16},{1,9},{9,1},{17,25},{25,17},{2,10},{10... | collective-permute-start | bytes 98312 | tf_op jit(solution)/shard_map/cond/branch_0_fun/ppermute | solution.py:293
  12.2 1.5 %collective-permute-start.1 = (f32[64,128]{1,0:T(8,128)S(1)}, f32[64,128]{1,0:T(8,128)S(1)}, u32[]{:S(2)}, u32[]{:S(2)}) collective-permute-start(f32[64,128]{1,0:T(8,128)S(1)} %get-tuple-element.37.own_ref.refs_2_), channel_id=1, source_target_pairs={{0,1},{1,0},{2,3},{3,2},{4,5},{5,4},{6,7},{7,6},{8,9},{9,8},{10,11... | collective-permute-start | bytes 98312 | tf_op jit(solution)/shard_map/cond/branch_0_fun/ppermute | solution.py:271
  13.8 0.6 %collective-permute-done.3 = f32[64,128]{1,0:T(8,128)S(1)} collective-permute-done((f32[64,128]{1,0:T(8,128)S(1)}, f32[64,128]{1,0:T(8,128)S(1)}, u32[]{:S(2)}, u32[]{:S(2)}) %collective-permute-start.3) | collective-permute-done | bytes 32800 | tf_op jit(solution)/shard_map/cond/branch_0_fun/ppermute | solution.py:293
  14.4 2.8 %collective-permute-start.4 = (f32[64,128]{1,0:T(8,128)S(1)}, f32[64,128]{1,0:T(8,128)S(1)}, u32[]{:S(2)}, u32[]{:S(2)}) collective-permute-start(f32[64,128]{1,0:T(8,128)S(1)} %add.12.left_ref), channel_id=1, source_target_pairs={{0,16},{8,24},{16,0},{24,8},{1,17},{9,25},{17,1},{25,9},{2,18},{10... | collective-permute-start | bytes 98312 | tf_op jit(solution)/shard_map/cond/branch_0_fun/ppermute | solution.py:293
  17.2 0.0 collective-permute-done.1.refs_3_
  17.2 0.8 %branch_0_fun.11.held_ref = bf16[1024,128]{1,0:T(8,128)(2,1)S(1)} custom-call(bf16[1024,128]{1,0:T(8,128)(2,1)S(1)} %collective-permute-done.refs_0_, bf16[1024,128]{1,0:T(8,128)(2,1)S(1)} %get-tuple-element.29.grad_ref.refs_1_, f32[64,128]{1,0:T(8,128)S(1)} %get-tuple-element.37.own_ref.refs_2_, f32[64,128]{1,0:T(8,128)S(1)} %collective-permute-done.1.refs_3_, ...), custom_call_target="tpu_custom_call" | custom-call | flops 536870912 | bytes 2097152 | tf_op jit(solution)/shard_map/cond/branch_0_fun/pallas_call | solution.py:207
  17.9 0.7 %branch_0_fun.12 = bf16[1024,128]{1,0:T(8,128)(2,1)} custom-call(bf16[1024,128]{1,0:T(8,128)(2,1)S(1)} %branch_0_fun.11.held_ref), custom_call_target="tpu_custom_call" | custom-call | flops 67108864 | bytes 262144 | tf_op jit(solution)/shard_map/cond/branch_0_fun/pallas_call | solution.py:207
  18.7 0.5 %collective-permute-done.4.right_ref = f32[64,128]{1,0:T(8,128)S(1)} collective-permute-done((f32[64,128]{1,0:T(8,128)S(1)}, f32[64,128]{1,0:T(8,128)S(1)}, u32[]{:S(2)}, u32[]{:S(2)}) %collective-permute-start.4) | collective-permute-done | bytes 32800 | tf_op jit(solution)/shard_map/cond/branch_0_fun/ppermute | solution.py:293
  19.2 0.6 %branch_0_fun.13 = f32[64,128]{1,0:T(8,128)} custom-call(f32[64,128]{1,0:T(8,128)S(1)} %add.12.left_ref, f32[64,128]{1,0:T(8,128)S(1)} %collective-permute-done.4.right_ref), custom_call_target="tpu_custom_call" | custom-call | flops 67108864 | bytes 262144 | tf_op jit(solution)/shard_map/cond/branch_0_fun/pallas_call | solution.py:207
  (2 shorter events, 0.0 us)
Async XLA Ops:
  0.7 4.2 %copy-start = (bf16[256,256]{1,0:T(8,128)(2,1)S(1)}, bf16[256,256]{1,0:T(8,128)(2,1)}, u32[]{:S(2)}) copy-start(bf16[256,256]{1,0:T(8,128)(2,1)} %get-tuple-element.32.forward_ref.refs_3_.refs_6_) | copy-start | bytes 393220 | tf_op jit(solution)/shard_map/cond
  0.7 4.2 %copy-start.2 = (bf16[256,256]{1,0:T(8,128)(2,1)S(1)}, bf16[256,256]{1,0:T(8,128)(2,1)}, u32[]{:S(2)}) copy-start(bf16[256,256]{1,0:T(8,128)(2,1)} %get-tuple-element.33.inverse_ref.refs_4_.refs_7_) | copy-start | bytes 393220 | tf_op jit(solution)/shard_map/cond
  1.9 7.9 %collective-permute-start = (bf16[1024,128]{1,0:T(8,128)(2,1)S(1)}, bf16[1024,128]{1,0:T(8,128)(2,1)S(1)}, u32[]{:S(2)}, u32[]{:S(2)}) collective-permute-start(bf16[1024,128]{1,0:T(8,128)(2,1)S(1)} %get-tuple-element.28), channel_id=1, source_target_pairs={{0,1},{1,0},{2,3},{3,2},{4,5},{5,4},{6,7},{7,6},{8,9},{9,8},{10,11... | collective-permute-start | bytes 786440 | tf_op jit(solution)/shard_map/cond/branch_0_fun/ppermute | solution.py:250
  5.5 4.9 %collective-permute-start.2 = (f32[64,128]{1,0:T(8,128)S(1)}, f32[64,128]{1,0:T(8,128)S(1)}, u32[]{:S(2)}, u32[]{:S(2)}) collective-permute-start(f32[64,128]{1,0:T(8,128)S(1)} %get-tuple-element.38), channel_id=1, source_target_pairs={{0,1},{1,0},{2,3},{3,2},{4,5},{5,4},{6,7},{7,6},{8,9},{9,8},{10,11... | collective-permute-start | bytes 98312 | tf_op jit(solution)/shard_map/cond/branch_0_fun/ppermute | solution.py:267
  10.4 4.0 %collective-permute-start.3 = (f32[64,128]{1,0:T(8,128)S(1)}, f32[64,128]{1,0:T(8,128)S(1)}, u32[]{:S(2)}, u32[]{:S(2)}) collective-permute-start(f32[64,128]{1,0:T(8,128)S(1)} %add.11), channel_id=1, source_target_pairs={{0,8},{8,0},{16,24},{24,16},{1,9},{9,1},{17,25},{25,17},{2,10},{10... | collective-permute-start | bytes 98312 | tf_op jit(solution)/shard_map/cond/branch_0_fun/ppermute | solution.py:293
  12.2 4.9 %collective-permute-start.1 = (f32[64,128]{1,0:T(8,128)S(1)}, f32[64,128]{1,0:T(8,128)S(1)}, u32[]{:S(2)}, u32[]{:S(2)}) collective-permute-start(f32[64,128]{1,0:T(8,128)S(1)} %get-tuple-element.37.own_ref.refs_2_), channel_id=1, source_target_pairs={{0,1},{1,0},{2,3},{3,2},{4,5},{5,4},{6,7},{7,6},{8,9},{9,8},{10,11... | collective-permute-start | bytes 98312 | tf_op jit(solution)/shard_map/cond/branch_0_fun/ppermute | solution.py:271
  14.4 4.8 %collective-permute-start.4 = (f32[64,128]{1,0:T(8,128)S(1)}, f32[64,128]{1,0:T(8,128)S(1)}, u32[]{:S(2)}, u32[]{:S(2)}) collective-permute-start(f32[64,128]{1,0:T(8,128)S(1)} %add.12.left_ref), channel_id=1, source_target_pairs={{0,16},{8,24},{16,0},{24,8},{1,17},{9,25},{17,1},{25,9},{2,18},{10... | collective-permute-start | bytes 98312 | tf_op jit(solution)/shard_map/cond/branch_0_fun/ppermute | solution.py:293

commit v3 on v2

--- a/solution.py
+++ b/solution.py
@@ -82,7 +82,7 @@
     return (1 - 2 * (lane % 2)).astype(jnp.float32)
 
 
-def local_lag(in_ref, grad_ref, forward_ref, inverse_ref, part_ref, lag_ref, taps_ref):
+def local_lag(in_ref, grad_ref, forward_ref, inverse_ref, part_ref, kept_ref, taps_ref, lag_ref):
     first = lax.axis_index("context") == 0
     chans, tok = in_ref.shape
     rows = block_rows(chans)
@@ -96,7 +96,9 @@
         lag_ref[groups, :tok] = group_sum(lag_re)
         lag_ref[groups, tok:] = group_sum(lag_im)
         part_ref[span, :] = jnp.where(first, in_spec, grad_spec)
-    taps_ref[...] = jnp.where(first, 0.0, inverse_float(lag_ref[...], inverse_ref[...]))
+    taps = inverse_float(lag_ref[...], inverse_ref[...])
+    kept_ref[...] = jnp.where(first, taps, 0.0)
+    taps_ref[...] = jnp.where(first, 0.0, taps)
 
 
 def local_corr(grad_ref, own_ref, skip_ref, forward_ref, inverse_ref, corr_ref, gained_ref, base_ref):
@@ -142,7 +144,7 @@
 
 
 def cross_lag_kernel(*refs):
-    *parts, part_ref, lag_ref, forward_ref, inverse_ref, out_ref, sum_ref = refs
+    *parts, part_ref, forward_ref, inverse_ref, out_ref, sum_ref = refs
     first = lax.axis_index("context") == 0
     chans, tok = part_ref.shape[0], out_ref.shape[1]
     rows = block_rows(chans)
@@ -158,8 +160,8 @@
     re, im = sum_ref[:, :tok], sum_ref[:, tok:]
     total = jnp.concatenate(
         [
-            jnp.where(first, lag_ref[:, :tok] + sign * im, re),
-            jnp.where(first, lag_ref[:, tok:] - sign * re, -im),
+            jnp.where(first, sign * im, re),
+            -jnp.where(first, sign * re, im),
         ],
         axis=1,
     )
@@ -248,10 +250,10 @@
     )
     own_in, own_grad, own, skip_held = loaded[-4:]
     moved = [lax.ppermute(loaded[0], "context", swap)]
-    part, lag, taps = call(
+    part, kept, taps = call(
         local_lag,
-        (pltpu.VMEM((chans, 2 * tok), jnp.float32), spectra, narrow),
-        [],
+        (pltpu.VMEM((chans, 2 * tok), jnp.float32), narrow, narrow),
+        [spectra],
         8 * cost,
         own_in, own_grad, forward, inverse,
     )
@@ -269,12 +271,12 @@
         corr, gained = correlate_local(own_grad)
         own, part, corr = lax.optimization_barrier((own, part, corr))
     other_filters = lax.ppermute(own, "context", swap)
-    total = other_taps + call(
+    total = (kept + other_taps) + call(
         cross_lag_kernel,
         narrow,
         [spectra],
         8 * cost,
-        *map(in_vmem, moved), part, lag, forward, inverse,
+        *map(in_vmem, moved), part, forward, inverse,
     )
 
     def correlate(filters):

time: 19.9 us -> 19.9 us (level)
  no operation moved by 1% of the time
where the time goes in v3:
time: 19.9 us; the launch traced here: 19.8 us
  starting transfers between devices  9.28 us (47%)
  Pallas kernels  5.13 us (26%)
  waiting for transfers between devices  4.64 us (23%)
  between operations  0.64 us (3%)
    pallas_call x7, Pallas kernels, call(): pl.pallas_call(kernel, out_shape=out_shape, in_specs=in_specs or [VMEM_SP...  5.13 us
    ppermute x2, starting transfers between devices, paired(): got = lax.ppermute(total, 'dp', [(i, i ^ step) for i in range(sequences)])  4.67 us
    ppermute x1, waiting for transfers between devices, paired(): moved = [lax.ppermute(loaded[0], 'context', swap)]  3.53 us
    ppermute x1, starting transfers between devices, paired(): moved = [lax.ppermute(loaded[0], 'context', swap)]  3.03 us
    ppermute x1, starting transfers between devices, paired(): other_filters = lax.ppermute(own, 'context', swap)  1.52 us
    ppermute x2, waiting for transfers between devices, paired(): got = lax.ppermute(total, 'dp', [(i, i ^ step) for i in range(sequences)])  1.11 us
  transfers between devices with their start and end apart: 5, of which 3 were waited for; matrix products, arithmetic and copies ran while one was open for 0% of the time, Pallas kernels for 17%

profile of v3, /device:TPU:0, one launch (start us, length us, event | category | flops | bytes accessed | tf_op | source)
XLA Modules:
  0.0 19.8 jit_solution(12382186766689174976)
XLA Ops:
  0.6 19.2 %conditional.1 = (bf16[1,1024,128]{2,1,0:T(8,128)(2,1)}, f32[64,128]{1,0:T(8,128)}) conditional(s32[]{:T(128)} %convert_element_type.3, (bf16[1,1024,128]{2,1,0:T(8,128)(2,1)}, bf16[1,1024,128]{2,1,0:T(8,128)(2,1)}, f32[1024]{0:T(1024)}, f32[64,128]{1,0:T(8,128)}, bf16[256,256]{1,0:T(8,128)(2,1)}, /*index=5*/bf16[256,256]{1,0:T(8,128)(2,1)}) %tuple.22, ...), branch_computations={%region_0.1_spmd, %region_1.2_spmd} | conditional | flops 2348834816 | bytes 12026168 | solution.py:459
  0.7 0.0 copy-start
  0.7 0.0 copy-start.2
  0.7 1.2 %branch_0_fun.7 = (bf16[1024,128]{1,0:T(8,128)(2,1)S(1)}, bf16[1024,128]{1,0:T(8,128)(2,1)S(1)}, bf16[1024,128]{1,0:T(8,128)(2,1)S(1)}, f32[64,128]{1,0:T(8,128)S(1)}, f32[8,128]{1,0:T(8,128)S(1)}) custom-call(bf16[1024,128]{1,0:T(8,128)(2,1)} %bitcast.8, bf16[1024,128]{1,0:T(8,128)(2,1)} %bitcast.10, f32[64,128]{1,0:T(8,128)} %get-tuple-element.26.filters_ref, ...), custom_call_target="tpu_custom_call" | custom-call | flops 67108864 | bytes 262144 | tf_op jit(solution)/shard_map/cond/branch_0_fun/pallas_call | solution.py:209
  1.9 3.0 %collective-permute-start = (bf16[1024,128]{1,0:T(8,128)(2,1)S(1)}, bf16[1024,128]{1,0:T(8,128)(2,1)S(1)}, u32[]{:S(2)}, u32[]{:S(2)}) collective-permute-start(bf16[1024,128]{1,0:T(8,128)(2,1)S(1)} %get-tuple-element.28), channel_id=1, source_target_pairs={{0,1},{1,0},{2,3},{3,2},{4,5},{5,4},{6,7},{7,6},{8,9},{9,8},{10,11... | collective-permute-start | bytes 786440 | tf_op jit(solution)/shard_map/cond/branch_0_fun/ppermute | solution.py:252
  4.9 0.0 copy-done
  4.9 0.0 copy-done.2
  4.9 0.6 %branch_0_fun.8 = (f32[1024,256]{1,0:T(8,128)S(1)}, f32[64,128]{1,0:T(8,128)S(1)}, f32[64,128]{1,0:T(8,128)S(1)}) custom-call(bf16[1024,128]{1,0:T(8,128)(2,1)S(1)} %get-tuple-element.31.in_ref, bf16[1024,128]{1,0:T(8,128)(2,1)S(1)} %get-tuple-element.29.grad_ref.refs_1_, bf16[256,256]{1,0:T(8,128)(2,1)S(1)} %copy-done, bf16[256,256]{1,0:T(8,128)(2,1)S(1)} %copy-done.2), custom_call_target="tpu_custom_call" | custom-call | flops 536870912 | bytes 2097152 | tf_op jit(solution)/shard_map/cond/branch_0_fun/pallas_call | solution.py:209
  5.5 0.0 collective-permute-start.2
  5.5 0.8 %branch_0_fun.9 = (f32[1024,128]{1,0:T(8,128)S(1)}, f32[1024,128]{1,0:T(8,128)S(1)}) custom-call(bf16[1024,128]{1,0:T(8,128)(2,1)S(1)} %get-tuple-element.29.grad_ref.refs_1_, f32[64,128]{1,0:T(8,128)S(1)} %get-tuple-element.37.own_ref.refs_2_, f32[8,128]{1,0:T(8,128)S(1)} %get-tuple-element.35.skip_ref, bf16[256,256]{1,0:T(8,128)(2,1)S(1)} %copy-done, ...), custom_call_target="tpu_custom_call" | custom-call | flops 536870912 | bytes 2097152 | tf_op jit(solution)/shard_map/cond/branch_0_fun/pallas_call | solution.py:209
  6.3 3.5 %collective-permute-done.refs_0_ = bf16[1024,128]{1,0:T(8,128)(2,1)S(1)} collective-permute-done((bf16[1024,128]{1,0:T(8,128)(2,1)S(1)}, bf16[1024,128]{1,0:T(8,128)(2,1)S(1)}, u32[]{:S(2)}, u32[]{:S(2)}) %collective-permute-start) | collective-permute-done | bytes 262176 | tf_op jit(solution)/shard_map/cond/branch_0_fun/ppermute | solution.py:252
  9.8 0.5 %branch_0_fun.10 = f32[64,128]{1,0:T(8,128)S(1)} custom-call(bf16[1024,128]{1,0:T(8,128)(2,1)S(1)} %collective-permute-done.refs_0_, f32[1024,256]{1,0:T(8,128)S(1)} %get-tuple-element.40.refs_1_, bf16[256,256]{1,0:T(8,128)(2,1)S(1)} %copy-done, bf16[256,256]{1,0:T(8,128)(2,1)S(1)} %copy-done.2), custom_call_target="tpu_custom_call" | custom-call | flops 536870912 | bytes 2097152 | tf_op jit(solution)/shard_map/cond/branch_0_fun/pallas_call | solution.py:209
  10.3 0.0 collective-permute-done.2
  10.4 1.9 %collective-permute-start.3 = (f32[64,128]{1,0:T(8,128)S(1)}, f32[64,128]{1,0:T(8,128)S(1)}, u32[]{:S(2)}, u32[]{:S(2)}) collective-permute-start(f32[64,128]{1,0:T(8,128)S(1)} %add_add_fusion), channel_id=1, source_target_pairs={{0,8},{8,0},{16,24},{24,16},{1,9},{9,1},{17,25},{25,17},{2,10},{10... | collective-permute-start | bytes 98312 | tf_op jit(solution)/shard_map/cond/branch_0_fun/ppermute | solution.py:295
  12.2 1.5 %collective-permute-start.1 = (f32[64,128]{1,0:T(8,128)S(1)}, f32[64,128]{1,0:T(8,128)S(1)}, u32[]{:S(2)}, u32[]{:S(2)}) collective-permute-start(f32[64,128]{1,0:T(8,128)S(1)} %get-tuple-element.37.own_ref.refs_2_), channel_id=1, source_target_pairs={{0,1},{1,0},{2,3},{3,2},{4,5},{5,4},{6,7},{7,6},{8,9},{9,8},{10,11... | collective-permute-start | bytes 98312 | tf_op jit(solution)/shard_map/cond/branch_0_fun/ppermute | solution.py:273
  13.8 0.6 %collective-permute-done.3 = f32[64,128]{1,0:T(8,128)S(1)} collective-permute-done((f32[64,128]{1,0:T(8,128)S(1)}, f32[64,128]{1,0:T(8,128)S(1)}, u32[]{:S(2)}, u32[]{:S(2)}) %collective-permute-start.3) | collective-permute-done | bytes 32800 | tf_op jit(solution)/shard_map/cond/branch_0_fun/ppermute | solution.py:295
  14.4 2.8 %collective-permute-start.4 = (f32[64,128]{1,0:T(8,128)S(1)}, f32[64,128]{1,0:T(8,128)S(1)}, u32[]{:S(2)}, u32[]{:S(2)}) collective-permute-start(f32[64,128]{1,0:T(8,128)S(1)} %add.17.left_ref), channel_id=1, source_target_pairs={{0,16},{8,24},{16,0},{24,8},{1,17},{9,25},{17,1},{25,9},{2,18},{10... | collective-permute-start | bytes 98312 | tf_op jit(solution)/shard_map/cond/branch_0_fun/ppermute | solution.py:295
  17.2 0.0 collective-permute-done.1.refs_3_
  17.2 0.8 %branch_0_fun.11.held_ref = bf16[1024,128]{1,0:T(8,128)(2,1)S(1)} custom-call(bf16[1024,128]{1,0:T(8,128)(2,1)S(1)} %collective-permute-done.refs_0_, bf16[1024,128]{1,0:T(8,128)(2,1)S(1)} %get-tuple-element.29.grad_ref.refs_1_, f32[64,128]{1,0:T(8,128)S(1)} %get-tuple-element.37.own_ref.refs_2_, f32[64,128]{1,0:T(8,128)S(1)} %collective-permute-done.1.refs_3_, ...), custom_call_target="tpu_custom_call" | custom-call | flops 536870912 | bytes 2097152 | tf_op jit(solution)/shard_map/cond/branch_0_fun/pallas_call | solution.py:209
  17.9 0.7 %branch_0_fun.12 = bf16[1024,128]{1,0:T(8,128)(2,1)} custom-call(bf16[1024,128]{1,0:T(8,128)(2,1)S(1)} %branch_0_fun.11.held_ref), custom_call_target="tpu_custom_call" | custom-call | flops 67108864 | bytes 262144 | tf_op jit(solution)/shard_map/cond/branch_0_fun/pallas_call | solution.py:209
  18.7 0.5 %collective-permute-done.4.right_ref = f32[64,128]{1,0:T(8,128)S(1)} collective-permute-done((f32[64,128]{1,0:T(8,128)S(1)}, f32[64,128]{1,0:T(8,128)S(1)}, u32[]{:S(2)}, u32[]{:S(2)}) %collective-permute-start.4) | collective-permute-done | bytes 32800 | tf_op jit(solution)/shard_map/cond/branch_0_fun/ppermute | solution.py:295
  19.2 0.6 %branch_0_fun.13 = f32[64,128]{1,0:T(8,128)} custom-call(f32[64,128]{1,0:T(8,128)S(1)} %add.17.left_ref, f32[64,128]{1,0:T(8,128)S(1)} %collective-permute-done.4.right_ref), custom_call_target="tpu_custom_call" | custom-call | flops 67108864 | bytes 262144 | tf_op jit(solution)/shard_map/cond/branch_0_fun/pallas_call | solution.py:209
  (2 shorter events, 0.0 us)
Async XLA Ops:
  0.7 4.2 %copy-start = (bf16[256,256]{1,0:T(8,128)(2,1)S(1)}, bf16[256,256]{1,0:T(8,128)(2,1)}, u32[]{:S(2)}) copy-start(bf16[256,256]{1,0:T(8,128)(2,1)} %get-tuple-element.32.forward_ref.refs_2_.refs_6_) | copy-start | bytes 393220 | tf_op jit(solution)/shard_map/cond
  0.7 4.2 %copy-start.2 = (bf16[256,256]{1,0:T(8,128)(2,1)S(1)}, bf16[256,256]{1,0:T(8,128)(2,1)}, u32[]{:S(2)}) copy-start(bf16[256,256]{1,0:T(8,128)(2,1)} %get-tuple-element.33.inverse_ref.refs_3_.refs_7_) | copy-start | bytes 393220 | tf_op jit(solution)/shard_map/cond
  1.9 7.9 %collective-permute-start = (bf16[1024,128]{1,0:T(8,128)(2,1)S(1)}, bf16[1024,128]{1,0:T(8,128)(2,1)S(1)}, u32[]{:S(2)}, u32[]{:S(2)}) collective-permute-start(bf16[1024,128]{1,0:T(8,128)(2,1)S(1)} %get-tuple-element.28), channel_id=1, source_target_pairs={{0,1},{1,0},{2,3},{3,2},{4,5},{5,4},{6,7},{7,6},{8,9},{9,8},{10,11... | collective-permute-start | bytes 786440 | tf_op jit(solution)/shard_map/cond/branch_0_fun/ppermute | solution.py:252
  5.5 4.9 %collective-permute-start.2 = (f32[64,128]{1,0:T(8,128)S(1)}, f32[64,128]{1,0:T(8,128)S(1)}, u32[]{:S(2)}, u32[]{:S(2)}) collective-permute-start(f32[64,128]{1,0:T(8,128)S(1)} %get-tuple-element.39), channel_id=1, source_target_pairs={{0,1},{1,0},{2,3},{3,2},{4,5},{5,4},{6,7},{7,6},{8,9},{9,8},{10,11... | collective-permute-start | bytes 98312 | tf_op jit(solution)/shard_map/cond/branch_0_fun/ppermute | solution.py:269
  10.4 4.0 %collective-permute-start.3 = (f32[64,128]{1,0:T(8,128)S(1)}, f32[64,128]{1,0:T(8,128)S(1)}, u32[]{:S(2)}, u32[]{:S(2)}) collective-permute-start(f32[64,128]{1,0:T(8,128)S(1)} %add_add_fusion), channel_id=1, source_target_pairs={{0,8},{8,0},{16,24},{24,16},{1,9},{9,1},{17,25},{25,17},{2,10},{10... | collective-permute-start | bytes 98312 | tf_op jit(solution)/shard_map/cond/branch_0_fun/ppermute | solution.py:295
  12.2 4.9 %collective-permute-start.1 = (f32[64,128]{1,0:T(8,128)S(1)}, f32[64,128]{1,0:T(8,128)S(1)}, u32[]{:S(2)}, u32[]{:S(2)}) collective-permute-start(f32[64,128]{1,0:T(8,128)S(1)} %get-tuple-element.37.own_ref.refs_2_), channel_id=1, source_target_pairs={{0,1},{1,0},{2,3},{3,2},{4,5},{5,4},{6,7},{7,6},{8,9},{9,8},{10,11... | collective-permute-start | bytes 98312 | tf_op jit(solution)/shard_map/cond/branch_0_fun/ppermute | solution.py:273
  14.4 4.8 %collective-permute-start.4 = (f32[64,128]{1,0:T(8,128)S(1)}, f32[64,128]{1,0:T(8,128)S(1)}, u32[]{:S(2)}, u32[]{:S(2)}) collective-permute-start(f32[64,128]{1,0:T(8,128)S(1)} %add.17.left_ref), channel_id=1, source_target_pairs={{0,16},{8,24},{16,0},{24,8},{1,17},{9,25},{17,1},{25,9},{2,18},{10... | collective-permute-start | bytes 98312 | tf_op jit(solution)/shard_map/cond/branch_0_fun/ppermute | solution.py:295

commit v4 on v3

--- a/solution.py
+++ b/solution.py
@@ -120,20 +120,33 @@
             gained_ref[pl.ds(start + at, tok), :] = gain * grad[at : at + tok, :].astype(jnp.float32)
 
 
-def load_kernel(in_ref, grad_ref, filters_ref, skip_ref, *refs):
+def load_kernel(whole, in_ref, grad_ref, filters_ref, skip_ref, *refs):
     first = lax.axis_index("context") == 0
-    *parts, in_held, grad_held, filters_held, skip_held, sems = refs
-    pairs = ((in_ref, in_held), (grad_ref, grad_held), (filters_ref, filters_held), (skip_ref, skip_held))
+    *parts, filters_held, skip_held, sems = refs
+    pairs = [(filters_ref, filters_held), (skip_ref, skip_held)]
+    if whole:
+        *parts, in_held, grad_held = parts
+        pairs += [(in_ref, in_held), (grad_ref, grad_held)]
     copies = [pltpu.make_async_copy(*pair, sems.at[i]) for i, pair in enumerate(pairs)]
+
+    def fetch(ref):
+        copy = pltpu.make_async_copy(ref, parts[0], sems.at[len(copies)])
+        copy.start()
+        copy.wait()
+
     for copy in copies:
         copy.start()
+    if not whole:
+        pl.when(first)(lambda: fetch(in_ref))
+        pl.when(jnp.logical_not(first))(lambda: fetch(grad_ref))
     for copy in copies:
         copy.wait()
-    start = 0
-    for part in parts:
-        span = pl.ds(start, part.shape[0])
-        part[...] = jnp.where(first, in_held[span, :], grad_held[span, :])
-        start += part.shape[0]
+    if whole:
+        start = 0
+        for part in parts:
+            span = pl.ds(start, part.shape[0])
+            part[...] = jnp.where(first, in_held[span, :], grad_held[span, :])
+            start += part.shape[0]
 
 
 def moved_block(parts, start, rows):
@@ -241,14 +254,16 @@
     sizes = (cut, chans - cut) if late else (chans,)
     parts = tuple(pltpu.VMEM((size, tok), jnp.bfloat16) for size in sizes)
     loaded = call(
-        load_kernel,
-        parts + (block, block, narrow, pltpu.VMEM(skip_rows.shape, jnp.float32)),
+        functools.partial(load_kernel, late),
+        parts + ((block, block) if late else ()) + (narrow, pltpu.VMEM(skip_rows.shape, jnp.float32)),
         [pltpu.SemaphoreType.DMA((4,))],
-        cost,
+        8 * cost,
         *(pltpu.with_memory_space_constraint(v, pltpu.HBM) for v in (own_in, own_grad, filters, skip_rows)),
         in_specs=[ANY_SPEC] * 4,
     )
-    own_in, own_grad, own, skip_held = loaded[-4:]
+    own, skip_held = loaded[-2:]
+    if late:
+        own_in, own_grad = loaded[2:4]
     moved = [lax.ppermute(loaded[0], "context", swap)]
     part, kept, taps = call(
         local_lag,

time: 19.9 us -> 20 us (level)
  no operation moved by 1% of the time
where the time goes in v4:
time: 20 us; the launch traced here: 19.9 us
  starting transfers between devices  9.29 us (46%)
  Pallas kernels  5.06 us (25%)
  waiting for transfers between devices  4.75 us (24%)
  between operations  0.64 us (3%)
    pallas_call x7, Pallas kernels, call(): pl.pallas_call(kernel, out_shape=out_shape, in_specs=in_specs or [VMEM_SP...  5.06 us
    ppermute x2, starting transfers between devices, paired(): got = lax.ppermute(total, 'dp', [(i, i ^ step) for i in range(sequences)])  4.67 us
    ppermute x1, waiting for transfers between devices, paired(): moved = [lax.ppermute(loaded[0], 'context', swap)]  3.59 us
    ppermute x1, starting transfers between devices, paired(): moved = [lax.ppermute(loaded[0], 'context', swap)]  3.03 us
    ppermute x1, starting transfers between devices, paired(): other_filters = lax.ppermute(own, 'context', swap)  1.51 us
    ppermute x2, waiting for transfers between devices, paired(): got = lax.ppermute(total, 'dp', [(i, i ^ step) for i in range(sequences)])  1.16 us
  transfers between devices with their start and end apart: 5, of which 3 were waited for; matrix products, arithmetic and copies ran while one was open for 0% of the time, Pallas kernels for 17%

profile of v4, /device:TPU:0, one launch (start us, length us, event | category | flops | bytes accessed | tf_op | source)
XLA Modules:
  0.0 19.9 jit_solution(6157414208924723547)
XLA Ops:
  0.6 19.2 %conditional.1 = (bf16[1,1024,128]{2,1,0:T(8,128)(2,1)}, f32[64,128]{1,0:T(8,128)}) conditional(s32[]{:T(128)} %convert_element_type.3, (bf16[1,1024,128]{2,1,0:T(8,128)(2,1)}, bf16[1,1024,128]{2,1,0:T(8,128)(2,1)}, f32[1024]{0:T(1024)}, f32[64,128]{1,0:T(8,128)}, bf16[256,256]{1,0:T(8,128)(2,1)}, /*index=5*/bf16[256,256]{1,0:T(8,128)(2,1)}) %tuple.22, ...), branch_computations={%region_0.1_spmd, %region_1.2_spmd} | conditional | flops 2818596864 | bytes 15958344 | solution.py:474
  0.7 0.0 copy-start
  0.7 0.0 copy-start.2
  0.7 0.0 copy-start.4
  0.7 0.0 copy-start.5
  0.7 1.1 %branch_0_fun.7 = (bf16[1024,128]{1,0:T(8,128)(2,1)S(1)}, f32[64,128]{1,0:T(8,128)S(1)}, f32[8,128]{1,0:T(8,128)S(1)}) custom-call(bf16[1024,128]{1,0:T(8,128)(2,1)} %bitcast.15, bf16[1024,128]{1,0:T(8,128)(2,1)} %bitcast.8, f32[64,128]{1,0:T(8,128)} %get-tuple-element.26.filters_ref, f32[8,128]{1,0:T(8,128)} %bitcast.18), custom_call_target="tpu_custom_call" | custom-call | flops 536870912 | bytes 2097152 | tf_op jit(solution)/shard_map/cond/branch_0_fun/pallas_call | solution.py:222
  1.8 3.0 %collective-permute-start = (bf16[1024,128]{1,0:T(8,128)(2,1)S(1)}, bf16[1024,128]{1,0:T(8,128)(2,1)S(1)}, u32[]{:S(2)}, u32[]{:S(2)}) collective-permute-start(bf16[1024,128]{1,0:T(8,128)(2,1)S(1)} %get-tuple-element.28), channel_id=1, source_target_pairs={{0,1},{1,0},{2,3},{3,2},{4,5},{5,4},{6,7},{7,6},{8,9},{9,8},{10,11... | collective-permute-start | bytes 786440 | tf_op jit(solution)/shard_map/cond/branch_0_fun/ppermute | solution.py:267
  4.8 0.0 copy-done
  4.8 0.0 copy-done.2
  4.8 0.0 copy-done.4
  4.8 0.0 copy-done.5
  4.9 0.6 %branch_0_fun.8 = (f32[1024,256]{1,0:T(8,128)S(1)}, f32[64,128]{1,0:T(8,128)S(1)}, f32[64,128]{1,0:T(8,128)S(1)}) custom-call(bf16[1024,128]{1,0:T(8,128)(2,1)S(1)} %bitcast.16, bf16[1024,128]{1,0:T(8,128)(2,1)S(1)} %bitcast.9, bf16[256,256]{1,0:T(8,128)(2,1)S(1)} %copy-done, bf16[256,256]{1,0:T(8,128)(2,1)S(1)} %copy-done.2), custom_call_target="tpu_custom_call" | custom-call | flops 536870912 | bytes 2097152 | tf_op jit(solution)/shard_map/cond/branch_0_fun/pallas_call | solution.py:222
  5.4 0.1 collective-permute-start.2
  5.5 0.8 %branch_0_fun.9 = (f32[1024,128]{1,0:T(8,128)S(1)}, f32[1024,128]{1,0:T(8,128)S(1)}) custom-call(bf16[1024,128]{1,0:T(8,128)(2,1)S(1)} %bitcast.10, f32[64,128]{1,0:T(8,128)S(1)} %get-tuple-element.35.own_ref.refs_2_, f32[8,128]{1,0:T(8,128)S(1)} %get-tuple-element.33.skip_ref, bf16[256,256]{1,0:T(8,128)(2,1)S(1)} %copy-done, bf16[256,256]{1,0:T(8,128)(2,1)S(1)} %copy-done.2), custom_call_target="tpu_custom_call" | custom-call | flops 536870912 | bytes 2097152 | tf_op jit(solution)/shard_map/cond/branch_0_fun/pallas_call | solution.py:222
  6.2 3.6 %collective-permute-done.refs_0_ = bf16[1024,128]{1,0:T(8,128)(2,1)S(1)} collective-permute-done((bf16[1024,128]{1,0:T(8,128)(2,1)S(1)}, bf16[1024,128]{1,0:T(8,128)(2,1)S(1)}, u32[]{:S(2)}, u32[]{:S(2)}) %collective-permute-start) | collective-permute-done | bytes 262176 | tf_op jit(solution)/shard_map/cond/branch_0_fun/ppermute | solution.py:267
  9.8 0.5 %branch_0_fun.10 = f32[64,128]{1,0:T(8,128)S(1)} custom-call(bf16[1024,128]{1,0:T(8,128)(2,1)S(1)} %collective-permute-done.refs_0_, f32[1024,256]{1,0:T(8,128)S(1)} %get-tuple-element.38.refs_1_, bf16[256,256]{1,0:T(8,128)(2,1)S(1)} %copy-done, bf16[256,256]{1,0:T(8,128)(2,1)S(1)} %copy-done.2), custom_call_target="tpu_custom_call" | custom-call | flops 536870912 | bytes 2097152 | tf_op jit(solution)/shard_map/cond/branch_0_fun/pallas_call | solution.py:222
  10.4 0.0 collective-permute-done.2
  10.4 1.9 %collective-permute-start.3 = (f32[64,128]{1,0:T(8,128)S(1)}, f32[64,128]{1,0:T(8,128)S(1)}, u32[]{:S(2)}, u32[]{:S(2)}) collective-permute-start(f32[64,128]{1,0:T(8,128)S(1)} %add_add_fusion), channel_id=1, source_target_pairs={{0,8},{8,0},{16,24},{24,16},{1,9},{9,1},{17,25},{25,17},{2,10},{10... | collective-permute-start | bytes 98312 | tf_op jit(solution)/shard_map/cond/branch_0_fun/ppermute | solution.py:310
  12.3 1.5 %collective-permute-start.1 = (f32[64,128]{1,0:T(8,128)S(1)}, f32[64,128]{1,0:T(8,128)S(1)}, u32[]{:S(2)}, u32[]{:S(2)}) collective-permute-start(f32[64,128]{1,0:T(8,128)S(1)} %get-tuple-element.35.own_ref.refs_2_), channel_id=1, source_target_pairs={{0,1},{1,0},{2,3},{3,2},{4,5},{5,4},{6,7},{7,6},{8,9},{9,8},{10,11... | collective-permute-start | bytes 98312 | tf_op jit(solution)/shard_map/cond/branch_0_fun/ppermute | solution.py:288
  13.8 0.6 %collective-permute-done.3 = f32[64,128]{1,0:T(8,128)S(1)} collective-permute-done((f32[64,128]{1,0:T(8,128)S(1)}, f32[64,128]{1,0:T(8,128)S(1)}, u32[]{:S(2)}, u32[]{:S(2)}) %collective-permute-start.3) | collective-permute-done | bytes 32800 | tf_op jit(solution)/shard_map/cond/branch_0_fun/ppermute | solution.py:310
  14.4 2.8 %collective-permute-start.4 = (f32[64,128]{1,0:T(8,128)S(1)}, f32[64,128]{1,0:T(8,128)S(1)}, u32[]{:S(2)}, u32[]{:S(2)}) collective-permute-start(f32[64,128]{1,0:T(8,128)S(1)} %add.17.left_ref), channel_id=1, source_target_pairs={{0,16},{8,24},{16,0},{24,8},{1,17},{9,25},{17,1},{25,9},{2,18},{10... | collective-permute-start | bytes 98312 | tf_op jit(solution)/shard_map/cond/branch_0_fun/ppermute | solution.py:310
  17.2 0.0 collective-permute-done.1.refs_3_
  17.2 0.8 %branch_0_fun.11.held_ref = bf16[1024,128]{1,0:T(8,128)(2,1)S(1)} custom-call(bf16[1024,128]{1,0:T(8,128)(2,1)S(1)} %collective-permute-done.refs_0_, bf16[1024,128]{1,0:T(8,128)(2,1)S(1)} %bitcast.11, f32[64,128]{1,0:T(8,128)S(1)} %get-tuple-element.35.own_ref.refs_2_, f32[64,128]{1,0:T(8,128)S(1)} %collective-permute-done.1.refs_3_, ...), custom_call_target="tpu_custom_call" | custom-call | flops 536870912 | bytes 2097152 | tf_op jit(solution)/shard_map/cond/branch_0_fun/pallas_call | solution.py:222
  18.0 0.7 %branch_0_fun.12 = bf16[1024,128]{1,0:T(8,128)(2,1)} custom-call(bf16[1024,128]{1,0:T(8,128)(2,1)S(1)} %branch_0_fun.11.held_ref), custom_call_target="tpu_custom_call" | custom-call | flops 67108864 | bytes 262144 | tf_op jit(solution)/shard_map/cond/branch_0_fun/pallas_call | solution.py:222
  18.7 0.6 %collective-permute-done.4.right_ref = f32[64,128]{1,0:T(8,128)S(1)} collective-permute-done((f32[64,128]{1,0:T(8,128)S(1)}, f32[64,128]{1,0:T(8,128)S(1)}, u32[]{:S(2)}, u32[]{:S(2)}) %collective-permute-start.4) | collective-permute-done | bytes 32800 | tf_op jit(solution)/shard_map/cond/branch_0_fun/ppermute | solution.py:310
  19.3 0.6 %branch_0_fun.13 = f32[64,128]{1,0:T(8,128)} custom-call(f32[64,128]{1,0:T(8,128)S(1)} %add.17.left_ref, f32[64,128]{1,0:T(8,128)S(1)} %collective-permute-done.4.right_ref), custom_call_target="tpu_custom_call" | custom-call | flops 67108864 | bytes 262144 | tf_op jit(solution)/shard_map/cond/branch_0_fun/pallas_call | solution.py:222
  (2 shorter events, 0.0 us)
Async XLA Ops:
  0.7 4.2 %copy-start = (bf16[256,256]{1,0:T(8,128)(2,1)S(1)}, bf16[256,256]{1,0:T(8,128)(2,1)}, u32[]{:S(2)}) copy-start(bf16[256,256]{1,0:T(8,128)(2,1)} %get-tuple-element.30.forward_ref.refs_2_.refs_6_) | copy-start | bytes 393220 | tf_op jit(solution)/shard_map/cond
  0.7 4.2 %copy-start.2 = (bf16[256,256]{1,0:T(8,128)(2,1)S(1)}, bf16[256,256]{1,0:T(8,128)(2,1)}, u32[]{:S(2)}) copy-start(bf16[256,256]{1,0:T(8,128)(2,1)} %get-tuple-element.31.inverse_ref.refs_3_.refs_7_) | copy-start | bytes 393220 | tf_op jit(solution)/shard_map/cond
  0.7 4.2 %copy-start.4 = (bf16[1,1024,128]{2,1,0:T(8,128)(2,1)S(1)}, bf16[1,1024,128]{2,1,0:T(8,128)(2,1)}, u32[]{:S(2)}) copy-start(bf16[1,1024,128]{2,1,0:T(8,128)(2,1)} %get-tuple-element.25) | copy-start | bytes 786436 | tf_op jit(solution)/shard_map/cond
  0.7 4.2 %copy-start.5 = (bf16[1,1024,128]{2,1,0:T(8,128)(2,1)S(1)}, bf16[1,1024,128]{2,1,0:T(8,128)(2,1)}, u32[]{:S(2)}) copy-start(bf16[1,1024,128]{2,1,0:T(8,128)(2,1)} %get-tuple-element.24) | copy-start | bytes 786436 | tf_op jit(solution)/shard_map/cond
  1.8 8.0 %collective-permute-start = (bf16[1024,128]{1,0:T(8,128)(2,1)S(1)}, bf16[1024,128]{1,0:T(8,128)(2,1)S(1)}, u32[]{:S(2)}, u32[]{:S(2)}) collective-permute-start(bf16[1024,128]{1,0:T(8,128)(2,1)S(1)} %get-tuple-element.28), channel_id=1, source_target_pairs={{0,1},{1,0},{2,3},{3,2},{4,5},{5,4},{6,7},{7,6},{8,9},{9,8},{10,11... | collective-permute-start | bytes 786440 | tf_op jit(solution)/shard_map/cond/branch_0_fun/ppermute | solution.py:267
  5.4 5.0 %collective-permute-start.2 = (f32[64,128]{1,0:T(8,128)S(1)}, f32[64,128]{1,0:T(8,128)S(1)}, u32[]{:S(2)}, u32[]{:S(2)}) collective-permute-start(f32[64,128]{1,0:T(8,128)S(1)} %get-tuple-element.37), channel_id=1, source_target_pairs={{0,1},{1,0},{2,3},{3,2},{4,5},{5,4},{6,7},{7,6},{8,9},{9,8},{10,11... | collective-permute-start | bytes 98312 | tf_op jit(solution)/shard_map/cond/branch_0_fun/ppermute | solution.py:284
  10.4 4.0 %collective-permute-start.3 = (f32[64,128]{1,0:T(8,128)S(1)}, f32[64,128]{1,0:T(8,128)S(1)}, u32[]{:S(2)}, u32[]{:S(2)}) collective-permute-start(f32[64,128]{1,0:T(8,128)S(1)} %add_add_fusion), channel_id=1, source_target_pairs={{0,8},{8,0},{16,24},{24,16},{1,9},{9,1},{17,25},{25,17},{2,10},{10... | collective-permute-start | bytes 98312 | tf_op jit(solution)/shard_map/cond/branch_0_fun/ppermute | solution.py:310
  12.3 4.9 %collective-permute-start.1 = (f32[64,128]{1,0:T(8,128)S(1)}, f32[64,128]{1,0:T(8,128)S(1)}, u32[]{:S(2)}, u32[]{:S(2)}) collective-permute-start(f32[64,128]{1,0:T(8,128)S(1)} %get-tuple-element.35.own_ref.refs_2_), channel_id=1, source_target_pairs={{0,1},{1,0},{2,3},{3,2},{4,5},{5,4},{6,7},{7,6},{8,9},{9,8},{10,11... | collective-permute-start | bytes 98312 | tf_op jit(solution)/shard_map/cond/branch_0_fun/ppermute | solution.py:288
  14.4 4.9 %collective-permute-start.4 = (f32[64,128]{1,0:T(8,128)S(1)}, f32[64,128]{1,0:T(8,128)S(1)}, u32[]{:S(2)}, u32[]{:S(2)}) collective-permute-start(f32[64,128]{1,0:T(8,128)S(1)} %add.17.left_ref), channel_id=1, source_target_pairs={{0,16},{8,24},{16,0},{24,8},{1,17},{9,25},{17,1},{25,9},{2,18},{10... | collective-permute-start | bytes 98312 | tf_op jit(solution)/shard_map/cond/branch_0_fun/ppermute | solution.py:310

commit v5 on v3

--- a/solution.py
+++ b/solution.py
@@ -266,10 +266,10 @@
         moved[0], rest, taps, part, own = lax.optimization_barrier((moved[0], loaded[1], taps, part, own, corr))[:5]
         moved.append(lax.ppermute(rest, "context", swap))
         taps, own = lax.optimization_barrier((taps, own))
-    other_taps = lax.ppermute(taps, "context", swap)
     if not late:
         corr, gained = correlate_local(own_grad)
-        own, part, corr = lax.optimization_barrier((own, part, corr))
+        own, part, corr, taps = lax.optimization_barrier((own, part, corr, taps))
+    other_taps = lax.ppermute(taps, "context", swap)
     other_filters = lax.ppermute(own, "context", swap)
     total = (kept + other_taps) + call(
         cross_lag_kernel,

time: 19.9 us -> 19.9 us (level)
  no operation moved by 1% of the time
where the time goes in v5:
time: 19.9 us; the launch traced here: 19.8 us
  starting transfers between devices  9.32 us (47%)
  Pallas kernels  5.14 us (26%)
  waiting for transfers between devices  4.59 us (23%)
  between operations  0.64 us (3%)
    pallas_call x7, Pallas kernels, call(): pl.pallas_call(kernel, out_shape=out_shape, in_specs=in_specs or [VMEM_SP...  5.14 us
    ppermute x2, starting transfers between devices, paired(): got = lax.ppermute(total, 'dp', [(i, i ^ step) for i in range(sequences)])  4.67 us
    ppermute x1, waiting for transfers between devices, paired(): moved = [lax.ppermute(loaded[0], 'context', swap)]  3.47 us
    ppermute x1, starting transfers between devices, paired(): moved = [lax.ppermute(loaded[0], 'context', swap)]  3.03 us
    ppermute x1, starting transfers between devices, paired(): other_filters = lax.ppermute(own, 'context', swap)  1.52 us
    ppermute x2, waiting for transfers between devices, paired(): got = lax.ppermute(total, 'dp', [(i, i ^ step) for i in range(sequences)])  1.11 us
  transfers between devices with their start and end apart: 5, of which 3 were waited for; matrix products, arithmetic and copies ran while one was open for 0% of the time, Pallas kernels for 17%

profile of v5, /device:TPU:0, one launch (start us, length us, event | category | flops | bytes accessed | tf_op | source)
XLA Modules:
  0.0 19.8 jit_solution(1480596999080179830)
XLA Ops:
  0.6 19.2 %conditional.1 = (bf16[1,1024,128]{2,1,0:T(8,128)(2,1)}, f32[64,128]{1,0:T(8,128)}) conditional(s32[]{:T(128)} %convert_element_type.3, (bf16[1,1024,128]{2,1,0:T(8,128)(2,1)}, bf16[1,1024,128]{2,1,0:T(8,128)(2,1)}, f32[1024]{0:T(1024)}, f32[64,128]{1,0:T(8,128)}, bf16[256,256]{1,0:T(8,128)(2,1)}, /*index=5*/bf16[256,256]{1,0:T(8,128)(2,1)}) %tuple.22, ...), branch_computations={%region_0.1_spmd, %region_1.2_spmd} | conditional | flops 2348834816 | bytes 12026168 | solution.py:459
  0.7 0.0 copy-start
  0.7 0.0 copy-start.2
  0.7 1.2 %branch_0_fun.7 = (bf16[1024,128]{1,0:T(8,128)(2,1)S(1)}, bf16[1024,128]{1,0:T(8,128)(2,1)S(1)}, bf16[1024,128]{1,0:T(8,128)(2,1)S(1)}, f32[64,128]{1,0:T(8,128)S(1)}, f32[8,128]{1,0:T(8,128)S(1)}) custom-call(bf16[1024,128]{1,0:T(8,128)(2,1)} %bitcast.8, bf16[1024,128]{1,0:T(8,128)(2,1)} %bitcast.10, f32[64,128]{1,0:T(8,128)} %get-tuple-element.26.filters_ref, ...), custom_call_target="tpu_custom_call" | custom-call | flops 67108864 | bytes 262144 | tf_op jit(solution)/shard_map/cond/branch_0_fun/pallas_call | solution.py:209
  1.9 3.0 %collective-permute-start = (bf16[1024,128]{1,0:T(8,128)(2,1)S(1)}, bf16[1024,128]{1,0:T(8,128)(2,1)S(1)}, u32[]{:S(2)}, u32[]{:S(2)}) collective-permute-start(bf16[1024,128]{1,0:T(8,128)(2,1)S(1)} %get-tuple-element.28), channel_id=1, source_target_pairs={{0,1},{1,0},{2,3},{3,2},{4,5},{5,4},{6,7},{7,6},{8,9},{9,8},{10,11... | collective-permute-start | bytes 786440 | tf_op jit(solution)/shard_map/cond/branch_0_fun/ppermute | solution.py:252
  4.9 0.0 copy-done
  4.9 0.0 copy-done.2
  4.9 0.6 %branch_0_fun.8 = (f32[1024,256]{1,0:T(8,128)S(1)}, f32[64,128]{1,0:T(8,128)S(1)}, f32[64,128]{1,0:T(8,128)S(1)}) custom-call(bf16[1024,128]{1,0:T(8,128)(2,1)S(1)} %get-tuple-element.31.in_ref, bf16[1024,128]{1,0:T(8,128)(2,1)S(1)} %get-tuple-element.29.grad_ref.refs_1_, bf16[256,256]{1,0:T(8,128)(2,1)S(1)} %copy-done, bf16[256,256]{1,0:T(8,128)(2,1)S(1)} %copy-done.2), custom_call_target="tpu_custom_call" | custom-call | flops 536870912 | bytes 2097152 | tf_op jit(solution)/shard_map/cond/branch_0_fun/pallas_call | solution.py:209
  5.5 0.8 %branch_0_fun.9 = (f32[1024,128]{1,0:T(8,128)S(1)}, f32[1024,128]{1,0:T(8,128)S(1)}) custom-call(bf16[1024,128]{1,0:T(8,128)(2,1)S(1)} %get-tuple-element.29.grad_ref.refs_1_, f32[64,128]{1,0:T(8,128)S(1)} %get-tuple-element.38.own_ref.refs_2_, f32[8,128]{1,0:T(8,128)S(1)} %get-tuple-element.35.skip_ref, bf16[256,256]{1,0:T(8,128)(2,1)S(1)} %copy-done, ...), custom_call_target="tpu_custom_call" | custom-call | flops 536870912 | bytes 2097152 | tf_op jit(solution)/shard_map/cond/branch_0_fun/pallas_call | solution.py:209
  6.2 0.1 collective-permute-start.2
  6.3 3.5 %collective-permute-done.refs_0_ = bf16[1024,128]{1,0:T(8,128)(2,1)S(1)} collective-permute-done((bf16[1024,128]{1,0:T(8,128)(2,1)S(1)}, bf16[1024,128]{1,0:T(8,128)(2,1)S(1)}, u32[]{:S(2)}, u32[]{:S(2)}) %collective-permute-start) | collective-permute-done | bytes 262176 | tf_op jit(solution)/shard_map/cond/branch_0_fun/ppermute | solution.py:252
  9.8 0.5 %branch_0_fun.10 = f32[64,128]{1,0:T(8,128)S(1)} custom-call(bf16[1024,128]{1,0:T(8,128)(2,1)S(1)} %collective-permute-done.refs_0_, f32[1024,256]{1,0:T(8,128)S(1)} %get-tuple-element.41.refs_1_, bf16[256,256]{1,0:T(8,128)(2,1)S(1)} %copy-done, bf16[256,256]{1,0:T(8,128)(2,1)S(1)} %copy-done.2), custom_call_target="tpu_custom_call" | custom-call | flops 536870912 | bytes 2097152 | tf_op jit(solution)/shard_map/cond/branch_0_fun/pallas_call | solution.py:209
  10.3 0.0 collective-permute-done.2
  10.4 1.9 %collective-permute-start.3 = (f32[64,128]{1,0:T(8,128)S(1)}, f32[64,128]{1,0:T(8,128)S(1)}, u32[]{:S(2)}, u32[]{:S(2)}) collective-permute-start(f32[64,128]{1,0:T(8,128)S(1)} %add_add_fusion), channel_id=1, source_target_pairs={{0,8},{8,0},{16,24},{24,16},{1,9},{9,1},{17,25},{25,17},{2,10},{10... | collective-permute-start | bytes 98312 | tf_op jit(solution)/shard_map/cond/branch_0_fun/ppermute | solution.py:295
  12.2 1.5 %collective-permute-start.1 = (f32[64,128]{1,0:T(8,128)S(1)}, f32[64,128]{1,0:T(8,128)S(1)}, u32[]{:S(2)}, u32[]{:S(2)}) collective-permute-start(f32[64,128]{1,0:T(8,128)S(1)} %get-tuple-element.38.own_ref.refs_2_), channel_id=1, source_target_pairs={{0,1},{1,0},{2,3},{3,2},{4,5},{5,4},{6,7},{7,6},{8,9},{9,8},{10,11... | collective-permute-start | bytes 98312 | tf_op jit(solution)/shard_map/cond/branch_0_fun/ppermute | solution.py:273
  13.8 0.6 %collective-permute-done.3 = f32[64,128]{1,0:T(8,128)S(1)} collective-permute-done((f32[64,128]{1,0:T(8,128)S(1)}, f32[64,128]{1,0:T(8,128)S(1)}, u32[]{:S(2)}, u32[]{:S(2)}) %collective-permute-start.3) | collective-permute-done | bytes 32800 | tf_op jit(solution)/shard_map/cond/branch_0_fun/ppermute | solution.py:295
  14.4 2.8 %collective-permute-start.4 = (f32[64,128]{1,0:T(8,128)S(1)}, f32[64,128]{1,0:T(8,128)S(1)}, u32[]{:S(2)}, u32[]{:S(2)}) collective-permute-start(f32[64,128]{1,0:T(8,128)S(1)} %add.17.left_ref), channel_id=1, source_target_pairs={{0,16},{8,24},{16,0},{24,8},{1,17},{9,25},{17,1},{25,9},{2,18},{10... | collective-permute-start | bytes 98312 | tf_op jit(solution)/shard_map/cond/branch_0_fun/ppermute | solution.py:295
  17.2 0.0 collective-permute-done.1.refs_3_
  17.2 0.8 %branch_0_fun.11.held_ref = bf16[1024,128]{1,0:T(8,128)(2,1)S(1)} custom-call(bf16[1024,128]{1,0:T(8,128)(2,1)S(1)} %collective-permute-done.refs_0_, bf16[1024,128]{1,0:T(8,128)(2,1)S(1)} %get-tuple-element.29.grad_ref.refs_1_, f32[64,128]{1,0:T(8,128)S(1)} %get-tuple-element.38.own_ref.refs_2_, f32[64,128]{1,0:T(8,128)S(1)} %collective-permute-done.1.refs_3_, ...), custom_call_target="tpu_custom_call" | custom-call | flops 536870912 | bytes 2097152 | tf_op jit(solution)/shard_map/cond/branch_0_fun/pallas_call | solution.py:209
  17.9 0.7 %branch_0_fun.12 = bf16[1024,128]{1,0:T(8,128)(2,1)} custom-call(bf16[1024,128]{1,0:T(8,128)(2,1)S(1)} %branch_0_fun.11.held_ref), custom_call_target="tpu_custom_call" | custom-call | flops 67108864 | bytes 262144 | tf_op jit(solution)/shard_map/cond/branch_0_fun/pallas_call | solution.py:209
  18.7 0.5 %collective-permute-done.4.right_ref = f32[64,128]{1,0:T(8,128)S(1)} collective-permute-done((f32[64,128]{1,0:T(8,128)S(1)}, f32[64,128]{1,0:T(8,128)S(1)}, u32[]{:S(2)}, u32[]{:S(2)}) %collective-permute-start.4) | collective-permute-done | bytes 32800 | tf_op jit(solution)/shard_map/cond/branch_0_fun/ppermute | solution.py:295
  19.2 0.6 %branch_0_fun.13 = f32[64,128]{1,0:T(8,128)} custom-call(f32[64,128]{1,0:T(8,128)S(1)} %add.17.left_ref, f32[64,128]{1,0:T(8,128)S(1)} %collective-permute-done.4.right_ref), custom_call_target="tpu_custom_call" | custom-call | flops 67108864 | bytes 262144 | tf_op jit(solution)/shard_map/cond/branch_0_fun/pallas_call | solution.py:209
  (2 shorter events, 0.0 us)
Async XLA Ops:
  0.7 4.2 %copy-start = (bf16[256,256]{1,0:T(8,128)(2,1)S(1)}, bf16[256,256]{1,0:T(8,128)(2,1)}, u32[]{:S(2)}) copy-start(bf16[256,256]{1,0:T(8,128)(2,1)} %get-tuple-element.32.forward_ref.refs_2_.refs_6_) | copy-start | bytes 393220 | tf_op jit(solution)/shard_map/cond
  0.7 4.2 %copy-start.2 = (bf16[256,256]{1,0:T(8,128)(2,1)S(1)}, bf16[256,256]{1,0:T(8,128)(2,1)}, u32[]{:S(2)}) copy-start(bf16[256,256]{1,0:T(8,128)(2,1)} %get-tuple-element.33.inverse_ref.refs_3_.refs_7_) | copy-start | bytes 393220 | tf_op jit(solution)/shard_map/cond
  1.9 7.9 %collective-permute-start = (bf16[1024,128]{1,0:T(8,128)(2,1)S(1)}, bf16[1024,128]{1,0:T(8,128)(2,1)S(1)}, u32[]{:S(2)}, u32[]{:S(2)}) collective-permute-start(bf16[1024,128]{1,0:T(8,128)(2,1)S(1)} %get-tuple-element.28), channel_id=1, source_target_pairs={{0,1},{1,0},{2,3},{3,2},{4,5},{5,4},{6,7},{7,6},{8,9},{9,8},{10,11... | collective-permute-start | bytes 786440 | tf_op jit(solution)/shard_map/cond/branch_0_fun/ppermute | solution.py:252
  6.2 4.1 %collective-permute-start.2 = (f32[64,128]{1,0:T(8,128)S(1)}, f32[64,128]{1,0:T(8,128)S(1)}, u32[]{:S(2)}, u32[]{:S(2)}) collective-permute-start(f32[64,128]{1,0:T(8,128)S(1)} %get-tuple-element.40), channel_id=1, source_target_pairs={{0,1},{1,0},{2,3},{3,2},{4,5},{5,4},{6,7},{7,6},{8,9},{9,8},{10,11... | collective-permute-start | bytes 98312 | tf_op jit(solution)/shard_map/cond/branch_0_fun/ppermute | solution.py:272
  10.4 4.0 %collective-permute-start.3 = (f32[64,128]{1,0:T(8,128)S(1)}, f32[64,128]{1,0:T(8,128)S(1)}, u32[]{:S(2)}, u32[]{:S(2)}) collective-permute-start(f32[64,128]{1,0:T(8,128)S(1)} %add_add_fusion), channel_id=1, source_target_pairs={{0,8},{8,0},{16,24},{24,16},{1,9},{9,1},{17,25},{25,17},{2,10},{10... | collective-permute-start | bytes 98312 | tf_op jit(solution)/shard_map/cond/branch_0_fun/ppermute | solution.py:295
  12.2 4.9 %collective-permute-start.1 = (f32[64,128]{1,0:T(8,128)S(1)}, f32[64,128]{1,0:T(8,128)S(1)}, u32[]{:S(2)}, u32[]{:S(2)}) collective-permute-start(f32[64,128]{1,0:T(8,128)S(1)} %get-tuple-element.38.own_ref.refs_2_), channel_id=1, source_target_pairs={{0,1},{1,0},{2,3},{3,2},{4,5},{5,4},{6,7},{7,6},{8,9},{9,8},{10,11... | collective-permute-start | bytes 98312 | tf_op jit(solution)/shard_map/cond/branch_0_fun/ppermute | solution.py:273
  14.4 4.8 %collective-permute-start.4 = (f32[64,128]{1,0:T(8,128)S(1)}, f32[64,128]{1,0:T(8,128)S(1)}, u32[]{:S(2)}, u32[]{:S(2)}) collective-permute-start(f32[64,128]{1,0:T(8,128)S(1)} %add.17.left_ref), channel_id=1, source_target_pairs={{0,16},{8,24},{16,0},{24,8},{1,17},{9,25},{17,1},{25,9},{2,18},{10... | collective-permute-start | bytes 98312 | tf_op jit(solution)/shard_map/cond/branch_0_fun/ppermute | solution.py:295
